TPU v7x, 32 devices: a whole 2x2x4 slice. The times are simulated.
32 devices in a mesh: seq: 8 (over y, x, core), tp: 4 (over z).
Axes of the slice: x: 2, y: 2, z: 4, core: 2. Of those that a mesh axis runs over, the one named last changes fastest.
Arguments:
- tokens: bfloat16 [1024, 16, 1024], P('seq', None, 'tp'), may hold values from -6 to 6
- norm_gain: bfloat16 [1024], P('tp'), may hold values from 0.5 to 1.5
- norm_shift: bfloat16 [1024], P('tp'), may hold values from -3 to 3
- query_weight: bfloat16 [1024, 1024], P(None, 'tp'), may hold values from -0.25 to 0.25
- key_weight: bfloat16 [1024, 1024], P(None, 'tp'), may hold values from -0.1875 to 0.1875
- value_weight: bfloat16 [1024, 1024], P(None, 'tp'), may hold values from -0.1875 to 0.1875
- output_weight: bfloat16 [1024, 1024], P('tp'), may hold values from -1 to 1
- inner_weight: bfloat16 [1024, 4096], P(None, 'tp'), may hold values from -0.1875 to 0.1875
- inner_bias: bfloat16 [4096], P('tp'), may hold values from -3 to 3
- outer_weight: bfloat16 [4096, 1024], P('tp'), may hold values from -0.09375 to 0.09375
- outer_bias: bfloat16 [1024], P('tp'), may hold values from -3 to 3
- lengths: int32 [16, 8], replicated, may hold values from 0 to 1024, as said below
- cotangent: bfloat16 [1024, 16, 1024], P('seq', None, 'tp'), may hold values from -6 to 6
Outputs:
- layer_out: bfloat16 [1024, 16, 1024], P('seq', None, 'tp')
- token_grad: float32 [1024, 16, 1024], P('seq', None, 'tp')
- gain_grad: float32 [1024], P('tp')
- shift_grad: float32 [1024], P('tp')
- query_weight_grad: float32 [1024, 1024], P(None, 'tp')
- key_weight_grad: float32 [1024, 1024], P(None, 'tp')
- value_weight_grad: float32 [1024, 1024], P(None, 'tp')
- output_weight_grad: float32 [1024, 1024], P('tp')
- inner_weight_grad: float32 [1024, 4096], P(None, 'tp')
- inner_bias_grad: float32 [4096], P('tp')
- outer_weight_grad: float32 [4096, 1024], P('tp')
- outer_bias_grad: float32 [1024], P('tp')
Inputs may be any that keep to these rules, and one draw needn't show every extreme that they name: Each row holds its proteins one after another from position 0 and padding after them; the lengths of a row sum to at most 1024; in one row a single protein fills all 1024 positions.
All inputs are finite; a program needn't handle non-finite values.
Results may differ from a plain program's by a relative error of at most 0.012.
Values may be sent and summed in bfloat16 or wider, within the bound.
No kernel may reach another device: no remote copies, remote signals or barrier semaphores. Data moves between devices by JAX's collectives and lax.ppermute only.
A program may use at most 320 MiB of HBM per device.

v0:
```python
from functools import partial

import jax
import jax.numpy as jnp
from jax import lax
from jax.sharding import PartitionSpec as P

DH = 64
ROTARY = 32
PROTEIN_SLOTS = 8


EPSILON = 1e-05
SCALING = 0.125
NEGATIVE = -1e30
BASE_FREQ = 10000.0


def packing_plan(lengths, extent):
    protein_ends = jnp.cumsum(lengths, axis=1)
    places = jnp.arange(extent, dtype=jnp.int32)
    passed = protein_ends[:, None, :] <= places[None, :, None]
    protein_segment = jnp.sum(passed.astype(jnp.int32), axis=2)
    begins = jnp.max(jnp.where(passed, protein_ends[:, None, :], 0), axis=2)
    padded = places[None, :] >= protein_ends[:, -1:]
    protein_segment = jnp.where(padded, PROTEIN_SLOTS + 1 + places[None, :], protein_segment)
    inside_position = jnp.where(padded, 0, places[None, :] - begins)
    return (protein_segment, inside_position)


def angles(inside_position):
    dim_index = jnp.arange(DH, dtype=jnp.int32)
    halves = (dim_index // 2).astype(jnp.float32)
    frequency = jnp.where(dim_index < ROTARY, BASE_FREQ ** (-2.0 * halves / ROTARY), 0.0)
    phase_angle = inside_position.astype(jnp.float32)[..., None] * frequency
    return (jnp.cos(phase_angle), jnp.sin(phase_angle))


def pair_turn(values):
    paired = values.reshape(values.shape[:-1] + (values.shape[-1] // 2, 2))
    return jnp.stack([-paired[..., 1], paired[..., 0]], axis=-1).reshape(values.shape)


def rotate(values, cosine_table, sine_table):
    return values * cosine_table + pair_turn(values) * sine_table


def visible(segment_rows, query_places, segment_cols, key_places):
    same_protein = (
        jnp.transpose(segment_rows)[:, :, None] == jnp.transpose(segment_cols)[:, None, :]
    )
    causal = query_places[:, None] >= key_places[None, :]
    return (same_protein & causal[None])[:, None]


def raw_scores(query_heads, key_heads):
    return (
        jnp.einsum("qrhd,krhd->rhqk", query_heads, key_heads, preferred_element_type=jnp.float32)
        * SCALING
    )


def softmax_weights(
    query_heads, segment_rows, query_places, key_heads, segment_cols, key_places, log_totals
):
    visible_mask = visible(segment_rows, query_places, segment_cols, key_places)
    scores = raw_scores(query_heads, key_heads)
    return jnp.where(
        visible_mask,
        jnp.exp(jnp.where(visible_mask, scores - log_totals[..., None], NEGATIVE)),
        0.0,
    )


def body(
    tokens,
    norm_gain,
    norm_shift,
    query_weight,
    key_weight,
    value_weight,
    output_weight,
    inner_weight,
    inner_bias,
    outer_weight,
    outer_bias,
    lengths,
    cotangent,
):
    shard_len, batch_rows, local_width = tokens.shape
    seq_count = lax.axis_size("seq")
    extent = shard_len * seq_count
    position = lax.axis_index("seq")
    width_index = lax.axis_index("tp")
    embed_width = query_weight.shape[1]
    heads_here = embed_width // DH
    protein_segment, inside_position = packing_plan(lengths, extent)
    segment_all = jnp.transpose(protein_segment)
    within_all = jnp.transpose(inside_position)
    first_row = position * shard_len
    last_row = first_row + shard_len - 1
    own_places = first_row + jnp.arange(shard_len, dtype=jnp.int32)
    own_segment = lax.dynamic_slice_in_dim(segment_all, first_row, shard_len, 0)
    own_within = lax.dynamic_slice_in_dim(within_all, first_row, shard_len, 0)
    cosine_table, sine_table = angles(own_within)
    cosine_table = cosine_table[:, :, None, :]
    sine_table = sine_table[:, :, None, :]
    key_span = min(512, extent)
    span_count = extent // key_span
    head_shape = (shard_len, batch_rows, heads_here, DH)

    def segment_slice(offset, amount):
        return lax.dynamic_slice_in_dim(segment_all, offset, amount, 0)

    def place_slice(offset, amount):
        return offset + jnp.arange(amount, dtype=jnp.int32)

    def key_block(history, offset):
        return lax.dynamic_slice_in_dim(history, offset, key_span, 0).reshape(
            key_span, batch_rows, heads_here, DH
        )

    whole_tokens, whole_gain, whole_shift = (
        lax.all_gather(tokens, "tp", axis=2, tiled=True),
        lax.all_gather(norm_gain, "tp", axis=0, tiled=True),
        lax.all_gather(norm_shift, "tp", axis=0, tiled=True),
    )
    widened = whole_tokens.astype(jnp.float32)
    centre = widened - jnp.mean(widened, axis=-1, keepdims=True)
    inverse = lax.rsqrt(jnp.mean(centre * centre, axis=-1, keepdims=True) + EPSILON)
    scaled = centre * inverse
    gain_full = whole_gain.astype(jnp.float32)
    hidden = (scaled * gain_full + whole_shift.astype(jnp.float32)).astype(jnp.bfloat16)

    def project(weight):
        return jnp.einsum("crd,de->cre", hidden, weight, preferred_element_type=jnp.float32)

    query_heads = rotate(
        project(query_weight).reshape(head_shape), cosine_table, sine_table
    ).astype(jnp.bfloat16)
    key_heads = rotate(project(key_weight).reshape(head_shape), cosine_table, sine_table).astype(
        jnp.bfloat16
    )
    value_heads = project(value_weight).astype(jnp.bfloat16).reshape(head_shape)
    key_rows = key_heads.reshape(shard_len, batch_rows, embed_width)
    value_rows = value_heads.reshape(shard_len, batch_rows, embed_width)
    key_hist, value_hist = (
        lax.all_gather(key_rows, "seq", axis=0, tiled=True),
        lax.all_gather(value_rows, "seq", axis=0, tiled=True),
    )

    def total_step(block_index, current):
        offset = block_index * key_span

        def total_accumulate(running):
            running_max, totals = running
            visible_mask = visible(
                own_segment,
                own_places,
                segment_slice(offset, key_span),
                place_slice(offset, key_span),
            )
            scores = jnp.where(
                visible_mask, raw_scores(query_heads, key_block(key_hist, offset)), NEGATIVE
            )
            new_max = jnp.maximum(running_max, jnp.max(scores, axis=-1))
            exp_terms = jnp.where(visible_mask, jnp.exp(scores - new_max[..., None]), 0.0)
            return (new_max, totals * jnp.exp(running_max - new_max) + jnp.sum(exp_terms, axis=-1))

        return lax.cond(offset <= last_row, total_accumulate, lambda running: running, current)

    stat_shape = (batch_rows, heads_here, shard_len)
    running_max, totals = lax.fori_loop(
        0,
        span_count,
        total_step,
        (jnp.full(stat_shape, NEGATIVE, jnp.float32), jnp.zeros(stat_shape, jnp.float32)),
    )
    log_totals = running_max + jnp.log(totals)

    def output_step(block_index, current):
        offset = block_index * key_span

        def output_accumulate(running):
            main_sum, low_sum = running
            weights = softmax_weights(
                query_heads,
                own_segment,
                own_places,
                key_block(key_hist, offset),
                segment_slice(offset, key_span),
                place_slice(offset, key_span),
                log_totals,
            )
            rounded = weights.astype(jnp.bfloat16)
            remainder = (weights - rounded.astype(jnp.float32)).astype(jnp.bfloat16)
            values_here = key_block(value_hist, offset)
            main_sum = main_sum + jnp.einsum(
                "rhqk,krhd->qrhd", rounded, values_here, preferred_element_type=jnp.float32
            )
            low_sum = low_sum + jnp.einsum(
                "rhqk,krhd->qrhd", remainder, values_here, preferred_element_type=jnp.float32
            )
            return (main_sum, low_sum)

        return lax.cond(offset <= last_row, output_accumulate, lambda running: running, current)

    zero_heads = jnp.zeros(head_shape, jnp.float32)
    main_sum, low_sum = lax.fori_loop(0, span_count, output_step, (zero_heads, zero_heads))
    mixed_exact = main_sum + low_sum
    mixed = main_sum.astype(jnp.bfloat16).reshape(shard_len, batch_rows, embed_width)
    inner = jnp.einsum(
        "crd,df->crf", hidden, inner_weight, preferred_element_type=jnp.float32
    ) + inner_bias.astype(jnp.float32)
    activated, gelu_back = jax.vjp(partial(jax.nn.gelu, approximate=True), inner)
    activated_low = activated.astype(jnp.bfloat16)
    branches = jnp.einsum(
        "cre,ed->crd", mixed, output_weight, preferred_element_type=jnp.float32
    ) + jnp.einsum("crf,fd->crd", activated_low, outer_weight, preferred_element_type=jnp.float32)
    branch_total = lax.psum_scatter(branches, "tp", scatter_dimension=2, tiled=True)
    layer_out = (tokens.astype(jnp.float32) + branch_total + outer_bias.astype(jnp.float32)).astype(
        jnp.bfloat16
    )
    grad_rows = lax.all_gather(cotangent, "tp", axis=2, tiled=True)
    outer_bias_grad = jnp.sum(cotangent.astype(jnp.float32), axis=(0, 1))
    output_grad = jnp.einsum("cre,crd->ed", mixed, grad_rows, preferred_element_type=jnp.float32)
    outer_grad = jnp.einsum(
        "crf,crd->fd", activated_low, grad_rows, preferred_element_type=jnp.float32
    )
    mixed_grad = (
        jnp.einsum("crd,ed->cre", grad_rows, output_weight, preferred_element_type=jnp.float32)
        .astype(jnp.bfloat16)
        .reshape(head_shape)
    )
    inner_grad_low = gelu_back(
        jnp.einsum("crd,fd->crf", grad_rows, outer_weight, preferred_element_type=jnp.float32)
    )[0].astype(jnp.bfloat16)
    inner_bias_grad = jnp.sum(inner_grad_low.astype(jnp.float32), axis=(0, 1))
    inner_grad = jnp.einsum(
        "crd,crf->df", hidden, inner_grad_low, preferred_element_type=jnp.float32
    )
    deltas = jnp.transpose(
        jnp.sum(mixed_grad.astype(jnp.float32) * mixed_exact, axis=-1), (1, 2, 0)
    )
    key_back, value_back = (
        lax.all_gather(key_rows, "seq", axis=0, tiled=True),
        lax.all_gather(value_rows, "seq", axis=0, tiled=True),
    )

    def query_step(block_index, current):
        offset = block_index * key_span

        def query_accumulate(running):
            keys_here = key_block(key_back, offset)
            values_here = key_block(value_back, offset)
            weights = softmax_weights(
                query_heads,
                own_segment,
                own_places,
                keys_here,
                segment_slice(offset, key_span),
                place_slice(offset, key_span),
                log_totals,
            )
            pushed = jnp.einsum(
                "qrhd,krhd->rhqk", mixed_grad, values_here, preferred_element_type=jnp.float32
            )
            score_grad = (weights * (pushed - deltas[..., None])).astype(jnp.bfloat16)
            return running + jnp.einsum(
                "rhqk,krhd->qrhd", score_grad, keys_here, preferred_element_type=jnp.float32
            )

        return lax.cond(offset <= last_row, query_accumulate, lambda running: running, current)

    query_grad_turned = lax.fori_loop(0, span_count, query_step, zero_heads) * SCALING
    offset = jnp.int32(0)
    amount = shard_len * lax.axis_size("seq")

    def compute(unused):
        keys_here = key_back.reshape(amount, batch_rows, heads_here, DH)
        values_here = value_back.reshape(amount, batch_rows, heads_here, DH)
        weights = softmax_weights(
            query_heads,
            own_segment,
            own_places,
            keys_here,
            segment_slice(offset, amount),
            place_slice(offset, amount),
            log_totals,
        )
        pushed = jnp.einsum(
            "qrhd,krhd->rhqk", mixed_grad, values_here, preferred_element_type=jnp.float32
        )
        score_grad = (weights * (pushed - deltas[..., None])).astype(jnp.bfloat16)
        key_part = (
            jnp.einsum(
                "rhqk,qrhd->krhd", score_grad, query_heads, preferred_element_type=jnp.float32
            )
            * SCALING
        )
        value_part = jnp.einsum(
            "rhqk,qrhd->krhd",
            weights.astype(jnp.bfloat16),
            mixed_grad,
            preferred_element_type=jnp.float32,
        )
        return jnp.concatenate(
            [
                key_part.reshape(amount, batch_rows, embed_width),
                value_part.reshape(amount, batch_rows, embed_width),
            ],
            axis=-1,
        )

    key_value_grads = lax.psum_scatter(
        lax.cond(
            offset <= last_row,
            compute,
            lambda unused: jnp.zeros((amount, batch_rows, 2 * embed_width), jnp.float32),
            0,
        ),
        "seq",
        scatter_dimension=0,
        tiled=True,
    )
    key_grad_turned = key_value_grads[..., :embed_width].reshape(head_shape)
    value_grad = key_value_grads[..., embed_width:]

    def unrotate(incoming):
        return incoming * cosine_table - pair_turn(incoming * sine_table)

    query_low = (
        unrotate(query_grad_turned).astype(jnp.bfloat16).reshape(shard_len, batch_rows, embed_width)
    )
    key_low = (
        unrotate(key_grad_turned).astype(jnp.bfloat16).reshape(shard_len, batch_rows, embed_width)
    )
    value_low = value_grad.astype(jnp.bfloat16)

    def weight_grad(incoming):
        return jnp.einsum("crd,cre->de", hidden, incoming, preferred_element_type=jnp.float32)

    def back_project(incoming, weight):
        return jnp.einsum("cre,de->crd", incoming, weight, preferred_element_type=jnp.float32)

    query_wgrad = weight_grad(query_low)
    key_wgrad = weight_grad(key_low)
    value_wgrad = weight_grad(value_low)
    hidden_grad = (
        back_project(query_low, query_weight)
        + back_project(key_low, key_weight)
        + back_project(value_low, value_weight)
        + back_project(inner_grad_low, inner_weight)
    )
    local_from = width_index * local_width
    scaled_here = lax.dynamic_slice_in_dim(scaled, local_from, local_width, 2)
    hidden_full = lax.psum(hidden_grad, "tp")
    gained = hidden_full * gain_full
    mean_one = jnp.mean(gained, axis=-1, keepdims=True)
    mean_two = jnp.mean(gained * scaled, axis=-1, keepdims=True)
    gained_here = lax.dynamic_slice_in_dim(gained, local_from, local_width, 2)
    hidden_here = lax.dynamic_slice_in_dim(hidden_full, local_from, local_width, 2)
    token_grad = cotangent.astype(jnp.float32) + inverse * (
        gained_here - mean_one - scaled_here * mean_two
    )
    gain_grad = jnp.sum(hidden_here * scaled_here, axis=(0, 1))
    shift_grad = jnp.sum(hidden_here, axis=(0, 1))
    reduced = lax.psum(
        (
            gain_grad,
            shift_grad,
            query_wgrad,
            key_wgrad,
            value_wgrad,
            output_grad,
            inner_grad,
            inner_bias_grad,
            outer_grad,
            outer_bias_grad,
        ),
        "seq",
    )
    return (
        layer_out,
        token_grad,
        reduced[0],
        reduced[1],
        reduced[2],
        reduced[3],
        reduced[4],
        reduced[5],
        reduced[6],
        reduced[7],
        reduced[8],
        reduced[9],
    )


def solution(mesh):
    return jax.shard_map(
        body,
        mesh=mesh,
        in_specs=(
            P("seq", None, "tp"),
            P("tp"),
            P("tp"),
            P(None, "tp"),
            P(None, "tp"),
            P(None, "tp"),
            P("tp", None),
            P(None, "tp"),
            P("tp"),
            P("tp", None),
            P("tp"),
            P(),
            P("seq", None, "tp"),
        ),
        out_specs=(
            P("seq", None, "tp"),
            P("seq", None, "tp"),
            P("tp"),
            P("tp"),
            P(None, "tp"),
            P(None, "tp"),
            P(None, "tp"),
            P("tp", None),
            P(None, "tp"),
            P("tp"),
            P("tp", None),
            P("tp"),
        ),
        check_vma=False,
    )
```

profile of v0, /device:TPU:0, one launch (start us, length us, event | category | flops | bytes accessed | tf_op | source)
XLA Modules:
  0.0 1368.9 jit_solution(17158749199792125090)
XLA Ops:
  13.3 12.7 all-gather
  48.9 44.6 %all-gather.7.cloned.1.call-done = bf16[128,16,1024]{2,0,1:T(8,128)(2,1)} async-done(((bf16[128,16,256]{2,0,1:T(8,128)(2,1)}), bf16[128,16,1024]{2,0,1:T(8,128)(2,1)}) %all-gather.7.cloned.1.call-update) | async-done | bytes 4194320 | tf_op jit(solution)/shard_map/all_gather | solution.py:124
  133.9 40.5 %all-gather.13.cloned.1.call-done = bf16[128,16,1024]{2,0,1:T(8,128)(2,1)} async-done(((bf16[128,16,256]{2,0,1:T(8,128)(2,1)}), bf16[128,16,1024]{2,0,1:T(8,128)(2,1)}) %all-gather.13.cloned.1.call-update) | async-done | bytes 4194320 | tf_op jit(solution)/shard_map/all_gather | solution.py:224
  184.0 45.5 %all-gather.11.cloned.1.call-done = bf16[1024,16,256]{2,0,1:T(8,128)(2,1)} async-done(((bf16[128,16,256]{2,0,1:T(8,128)(2,1)}), bf16[1024,16,256]{2,0,1:T(8,128)(2,1)}) %all-gather.11.cloned.1.call-update) | async-done | bytes 8388624 | tf_op jit(solution)/shard_map/all_gather | solution.py:148
  241.9 20.7 %while.49 = (s32[]{:T(128)}, f32[16,4,128]{2,1,0:T(4,128)S(1)}, f32[16,4,128]{2,1,0:T(4,128)S(1)}, s32[]{:T(128)}, s32[128,16]{0,1:T(8,128)S(1)}, /*index=5*/s32...) while((s32[]{:T(128)}, f32[16,4,128]{2,1,0:T(4,128)S(1)}, ...), condition=%wide.region_10.11_spmd.clone, body=%wide.region_5.10_spmd.clone.sunk | while | flops 572605056 | bytes 51001640 | solution.py:173
  241.9 20.6 %conditional.11 = ((f32[16,4,128]{2,1,0:T(4,128)S(1)}, f32[16,4,128]{2,1,0:T(4,128)S(1)})) conditional(s32[]{:T(128)} %convert_element_type.251, (f32[16,4,128]{2,1,0:T(4,128)S(1)}, f32[16,4,128]{2,1,0:T(4,128)S(1)}) %tuple.167, (s32[128,16]{0,1:T(8,128)S(1)}, s32[]{:T(128)}, s32[1024,16]{0,1:T(8,128)S(1)}, s32[]{:T(128)}, ...), branch_computations={%region_6.6_spmd, %region_7.9_spmd} | conditional | flops 572605056 | bytes 51000904 | solution.py:170
  262.6 23.7 %all-gather.9.cloned.1.call-done = bf16[1024,16,256]{2,0,1:T(8,128)(2,1)} async-done(((bf16[128,16,256]{2,0,1:T(8,128)(2,1)}), bf16[1024,16,256]{2,0,1:T(8,128)(2,1)}) %all-gather.9.cloned.1.call-update) | async-done | bytes 8388624 | tf_op jit(solution)/shard_map/all_gather | solution.py:149
  301.7 34.3 %while.50 = (s32[]{:T(128)}, f32[128,16,4,64]{0,3,2,1:T(8,128)}, f32[128,16,4,64]{0,3,2,1:T(8,128)}, s32[]{:T(128)}, bf16[1024,16,256]{0,2,1:T(8,128)(2,1)}, /*i...) while((s32[]{:T(128)}, f32[128,16,4,64]{0,3,2,1:T(8,128)}, ...), condition=%wide.region_14.15_spmd.clone, body=%wide.region_11.14_spmd.clone.sunk | while | flops 1668350592 | bytes 109361536 | solution.py:209
  302.1 33.9 %conditional.12 = ((f32[128,16,4,64]{0,3,2,1:T(8,128)}, f32[128,16,4,64]{0,3,2,1:T(8,128)})) conditional(s32[]{:T(128)} %convert_element_type.252, (f32[128,16,4,64]{0,3,2,1:T(8,128)}, f32[128,16,4,64]{0,3,2,1:T(8,128)}) %tuple.170, (s32[]{:T(128)}, bf16[1024,16,256]{0,2,1:T(8,128)(2,1)}, s32[128,16]{0,1:T(8,128)S(1)}, s32[1024,16]{0,1:T(8,128)S(1)}, ...), branch_computations={%region_12.12_spmd, %region_13.13_spmd} | conditional | flops 1668350592 | bytes 109360768 | solution.py:206
  341.6 113.5 %conditional.4 = (f32[1024,16,512]{0,2,1:T(8,128)}) conditional(s32[]{:T(128)} %convert_element_type.146, () %tuple.83, (s32[128,16]{0,1:T(8,128)S(1)}, s32[16,1024]{1,0:T(8,128)S(1)}, s32[]{:T(128)}, bf16[1024,16,256]{2,0,1:T(8,128)(2,1)}, bf16[128,16,4,64]{0,3,2,1:T(8,128)(2,1)S(1)}, /*index=5*/f32[16,4,128]{2,1,0:T(4,128)S(1)}, ...), branch_computations={%region_21.22_spmd, %region_22.23_spmd} | conditional | flops 4412538880 | bytes 329688608 | solution.py:316
  354.0 19.0 %fusion.95 = f32[16,4,128,1024]{3,2,1,0:T(8,128)} fusion(bf16[128,16,4,64]{0,3,2,1:T(8,128)(2,1)S(1)} %get-tuple-element.673, bf16[1024,16,4,64]{0,3,2,1:T(8,128)(2,1)} %bitcast.190), kind=kOutput, calls=%fused_computation.192 | convolution fusion | flops 1073741824 | bytes 42991616 | tf_op jit(solution)/shard_map/cond/branch_1_fun/qrhd,krhd->rhqk/dot_general | solution.py:58
  388.0 25.9 %fusion.42 = f32[16,4,1024,64]{2,3,1,0:T(8,128)} fusion(bf16[128,16,4,64]{0,3,2,1:T(8,128)(2,1)S(1)} %get-tuple-element.673, f32[16,4,128,1024]{3,2,1,0:T(8,128)} %fusion.95, f32[16,4,128]{2,1,0:T(4,128)} %get-tuple-element.678, f32[16,4,128]{2,1,0:T(4,128)S(1)} %get-tuple-element.675, bf16[128,16,4,64]{0,3,2,1:T(8,128)(2,1)} %get-tuple-element.676, ...), kind=kOutput, calls=%fused_computation.66 | convolution fusion | flops 2210398208 | bytes 62980096 | tf_op jit(solution)/shard_map/cond/branch_1_fun/rhqk,qrhd->krhd/dot_general | solution.py:296
  413.9 20.9 %fusion.31 = f32[16,4,1024,64]{2,3,1,0:T(8,128)} fusion(bf16[128,16,4,64]{0,3,2,1:T(8,128)(2,1)} %get-tuple-element.676, f32[16,4,128,1024]{3,2,1,0:T(8,128)} %fusion.95, f32[16,4,128]{2,1,0:T(4,128)S(1)} %get-tuple-element.675, pred[16,128,1024]{2,1,0:T(8,128)(4,1)} %compare_and_fusion.3), kind=kOutput, calls=%fused_computation.57 | convolution fusion | flops 1115684864 | bytes 53510144 | tf_op jit(solution)/shard_map/cond/branch_1_fun/rhqk,qrhd->krhd/dot_general | solution.py:301
  436.1 19.0 %pad_maximum_fusion = f32[1024,16,512]{0,2,1:T(8,128)} fusion(f32[1024,16,256]{0,2,1:T(8,128)} %bitcast.194, f32[1024,16,256]{0,2,1:T(8,128)S(1)} %bitcast.193), kind=kLoop, calls=%fused_computation.53 | loop fusion | flops 8388608 | bytes 67108864 | tf_op jit(solution)/shard_map/cond/branch_1_fun/concatenate | solution.py:307
  455.1 31.9 %copy.162 = f32[1024,16,512]{2,0,1:T(8,128)} copy(f32[1024,16,512]{0,2,1:T(8,128)} %get-tuple-element.1453) | data formatting | bytes 67108864 | tf_op jit(solution)/shard_map/cond | solution.py:316
  509.0 13.4 convert_reduce_fusion.1
  530.9 41.4 %while.51 = (s32[]{:T(128)}, f32[128,16,4,64]{0,3,2,1:T(8,128)}, s32[]{:T(128)}, bf16[1024,16,256]{0,2,1:T(8,128)(2,1)}, s32[128,16]{0,1:T(8,128)S(1)}, /*index=...) while((s32[]{:T(128)}, f32[128,16,4,64]{0,3,2,1:T(8,128)}, ...), condition=%wide.region_20.21_spmd.clone, body=%wide.region_17.20_spmd.clone.sunk | while | flops 1642660480 | bytes 88389976 | solution.py:275
  530.9 41.2 %conditional.13 = (f32[128,16,4,64]{0,3,2,1:T(8,128)}) conditional(s32[]{:T(128)} %convert_element_type.253, f32[128,16,4,64]{0,3,2,1:T(8,128)} %get-tuple-element.1408, (s32[]{:T(128)}, bf16[1024,16,256]{0,2,1:T(8,128)(2,1)}, s32[128,16]{0,1:T(8,128)S(1)}, s32[1024,16]{0,1:T(8,128)S(1)}, s32[]{:T(128)}, ...), branch_computations={%region_18.18_spmd, %region_19.19_spmd} | conditional | flops 1642660480 | bytes 88389208 | solution.py:273
  552.1 20.0 %bitcast_add_fusion.2 = f32[128,16,4,64]{0,3,2,1:T(8,128)} fusion(f32[128,16,4,64]{0,3,2,1:T(8,128)} %get-tuple-element.646, bf16[512,16,4,64]{0,3,2,1:T(8,128)(2,1)} %bitcast.184, f32[16,4,512,128]{3,2,1,0:T(8,128)} %fusion.94, bf16[512,16,4,64]{0,3,2,1:T(8,128)(2,1)} %bitcast.189, bf16[128,16,4,64]{0,3,2,1:T(8,128)(2,1)} %get-tuple-element.655, ...), kind=kOutput, calls=%fused_computation.43 | convolution fusion | flops 1103626240 | bytes 31522816 | tf_op jit(solution)/shard_map/while/body/eval_jaxpr/cond/branch_1_fun/rhqk,krhd->qrhd/dot_general | solution.py:269
  585.0 141.4 %reduce-scatter.5.cloned.1.call-done = f32[128,16,512]{2,0,1:T(8,128)} async-done(((f32[1024,16,512]{2,0,1:T(8,128)}), f32[128,16,512]{2,0,1:T(8,128)}) %reduce-scatter.5.cloned.1.call-update) | async-done | bytes 4194320 | tf_op jit(solution)/shard_map/reduce_scatter | solution.py:315
  796.7 76.5 %reduce-scatter.3.cloned.1.call-done = f32[128,16,256]{2,0,1:T(8,128)} async-done(((f32[128,16,1024]{2,0,1:T(8,128)}), f32[128,16,256]{2,0,1:T(8,128)}) %reduce-scatter.3.cloned.1.call-update) | async-done | bytes 2097168 | tf_op jit(solution)/shard_map/reduce_scatter | solution.py:220
  876.7 290.6 %all-reduce.5.cloned.1.call-done = f32[128,16,1024]{2,0,1:T(8,128)} async-done(((f32[128,16,1024]{2,0,1:T(8,128)}), f32[128,16,1024]{2,0,1:T(8,128)}) %all-reduce.5.cloned.1.call-update) | async-done | bytes 8388624 | tf_op jit(solution)/shard_map/psum | solution.py:357
  1178.8 15.5 %all-reduce = (f32[256]{0:T(256)}, f32[256]{0:T(256)}, f32[1024]{0:T(1024)}, f32[256]{0:T(256)}) all-reduce(f32[256]{0:T(256)S(1)} %get-tuple-element.1003, f32[256]{0:T(256)S(1)} %get-tuple-element.1002, f32[1024]{0:T(1024)S(1)} %copy-done.43, f32[256]{0:T(256)S(1)} %get-tuple-element.1101), channel_id=1, replica_groups=mesh['seq'=8,'tp'=4] {'seq'}, use_global_device_ids=true, to_apply=%region_28.29 | all-reduce | flops 1792 | bytes 14336 | tf_op jit(solution)/shard_map/psum | solution.py:368
  1194.3 153.3 %all-reduce.7.cloned.1.call-done = (f32[1024,256]{1,0:T(8,128)}, f32[1024,256]{1,0:T(8,128)}, f32[1024,256]{1,0:T(8,128)}, f32[256,1024]{1,0:T(8,128)}, f32[1024,1024]{1,0:T(8,128)}, /*index=5*/f32[1024,1024]{1,0:T(8,128)}) async-done(((f32[1024,256]{1,0:T(8,128)}, f32[1024,256]{1,0:T(8,128)}, f32[1024,256]{1,0:T(8,128)}, f32[256,1024]{1,0:T(8,128)}, f32[1024,1024]{1,0:T(8,128)}, ...) | async-done | bytes 12582928 | tf_op jit(solution)/shard_map/psum | solution.py:368
  (264 shorter events, 358.4 us)
Async XLA Ops:
  7.2 487.7 %copy-start = (bf16[1024,1024]{1,0:T(8,128)(2,1)S(1)}, bf16[1024,1024]{1,0:T(8,128)(2,1)}, u32[]{:S(2)}) copy-start(bf16[1024,1024]{1,0:T(8,128)(2,1)} %param.36) | copy-start | bytes 6291460
  7.2 86.3 %all-gather.7.cloned.1.call-start = ((), (), s32[]{:S(2)}) async-start(), calls=%async_computation.2 | async-start | bytes 5242880 | tf_op jit(solution)/shard_map/all_gather | solution.py:124
  9.9 164.5 %all-gather.13.cloned.1.call-start = ((), (), s32[]{:S(2)}) async-start(), calls=%async_computation.6 | async-start | bytes 5242880 | tf_op jit(solution)/shard_map/all_gather | solution.py:224
  12.5 217.0 %all-gather.11.cloned.1.call-start = ((), (), s32[]{:S(2)}) async-start(), calls=%async_computation.4 | async-start | bytes 9437184 | tf_op jit(solution)/shard_map/all_gather | solution.py:148
  26.0 96.5 %copy-start.40 = (f32[4,1,256]{2,1,0:T(1,128)}, f32[4,1,256]{2,1,0:T(1,128)S(1)}, u32[]{:S(2)}) copy-start(f32[4,1,256]{2,1,0:T(1,128)S(1)} %convert_element_type.151) | copy-start | bytes 12292
  34.3 88.2 %copy-start.46 = (f32[4,1,256]{2,1,0:T(1,128)}, f32[4,1,256]{2,1,0:T(1,128)S(1)}, u32[]{:S(2)}) copy-start(f32[4,1,256]{2,1,0:T(1,128)S(1)} %convert_element_type.152) | copy-start | bytes 12292
  39.1 57.4 %copy-start.13 = (f32[128,16,64]{0,2,1:T(8,128)}, f32[128,16,64]{0,2,1:T(8,128)S(1)}, u32[]{:S(2)}) copy-start(f32[128,16,64]{0,2,1:T(8,128)S(1)} %get-tuple-element.1104) | copy-start | bytes 1572868
  44.4 55.2 %copy-start.29 = (bf16[1024,256]{1,0:T(8,128)(2,1)S(1)}, bf16[1024,256]{1,0:T(8,128)(2,1)}, u32[]{:S(2)}) copy-start(bf16[1024,256]{1,0:T(8,128)(2,1)} %param.31) | copy-start | bytes 1572868
  96.5 26.0 %copy-start.35 = (f32[128,16]{0,1:T(8,128)}, f32[128,16]{0,1:T(8,128)S(1)}, u32[]{:S(2)}) copy-start(f32[128,16]{0,1:T(8,128)S(1)} %broadcast_multiply_fusion.7) | copy-start | bytes 24580
  99.5 23.0 %copy-start.32 = (f32[128,16]{0,1:T(8,128)}, f32[128,16]{0,1:T(8,128)S(1)}, u32[]{:S(2)}) copy-start(f32[128,16]{0,1:T(8,128)S(1)} %add_rsqrt_fusion) | copy-start | bytes 24580
  116.9 169.4 %all-gather.9.cloned.1.call-start = ((), (), s32[]{:S(2)}) async-start(), calls=%async_computation.3 | async-start | bytes 9437184 | tf_op jit(solution)/shard_map/all_gather | solution.py:149
  122.1 604.3 %reduce-scatter.5.cloned.1.call-start = ((), (), s32[]{:S(2)}) async-start(), calls=%async_computation.7 | async-start | bytes 37748736 | tf_op jit(solution)/shard_map/reduce_scatter | solution.py:315
  301.7 39.9 %copy-start.31 = (s32[16,1024]{1,0:T(8,128)S(1)}, s32[16,1024]{1,0:T(8,128)}, u32[]{:S(2)}) copy-start(s32[16,1024]{1,0:T(8,128)} %copy-done.30) | copy-start | bytes 196612
  413.9 22.3 %copy-start.5 = (f32[16,4,1024,64]{2,3,1,0:T(8,128)S(1)}, f32[16,4,1024,64]{2,3,1,0:T(8,128)}, u32[]{:S(2)}) copy-start(f32[16,4,1024,64]{2,3,1,0:T(8,128)} %fusion.42) | copy-start | bytes 50331652 | tf_op jit(solution)/shard_map/cond
  487.1 386.1 %reduce-scatter.3.cloned.1.call-start = ((), (), s32[]{:S(2)}) async-start(), calls=%async_computation.5 | async-start | bytes 10485760 | tf_op jit(solution)/shard_map/reduce_scatter | solution.py:220
  487.8 21.2 %copy-start.44 = (f32[1024]{0:T(1024)}, f32[1024]{0:T(1024)S(1)}, u32[]{:S(2)}) copy-start(f32[1024]{0:T(1024)S(1)} %convert_element_type.138) | copy-start | bytes 12292
  505.3 662.1 %all-reduce.5.cloned.1.call-start = ((), (), s32[]{:S(2)}) async-start(), calls=%async_computation.8 | async-start | bytes 16777216 | tf_op jit(solution)/shard_map/psum | solution.py:357
  509.0 13.4 copy-start.51
  580.4 152.1 %copy-start.23 = (f32[128,16,32,2]{0,1,3,2:T(8,128)S(1)}, f32[128,16,32,2]{0,1,3,2:T(8,128)}, u32[]{:S(2)}) copy-start(f32[128,16,32,2]{0,1,3,2:T(8,128)} %multiply_sine_fusion.1) | copy-start | bytes 1572868
  760.2 587.4 %all-reduce.7.cloned.1.call-start = ((), (), s32[]{:S(2)}) async-start(), calls=%async_computation.9 | async-start | bytes 25165824 | tf_op jit(solution)/shard_map/psum | solution.py:368
  771.4 13.9 %copy-start.3 = (bf16[128,16,1024]{2,0,1:T(8,128)(2,1)S(1)}, bf16[128,16,1024]{2,0,1:T(8,128)(2,1)}, u32[]{:S(2)}) copy-start(bf16[128,16,1024]{2,0,1:T(8,128)(2,1)} %all-gather.7.cloned.1.call-done) | copy-start | bytes 12582916
  771.4 13.9 %copy-start.22 = (bf16[128,16,4,64]{0,3,2,1:T(8,128)(2,1)S(1)}, bf16[128,16,4,64]{0,3,2,1:T(8,128)(2,1)}, u32[]{:S(2)}) copy-start(bf16[128,16,4,64]{0,3,2,1:T(8,128)(2,1)} %copy-done.21) | copy-start | bytes 3145732
  796.0 77.1 %copy-start.15 = (bf16[128,16,256]{2,1,0:T(8,128)(2,1)S(1)}, bf16[128,16,256]{2,1,0:T(8,128)(2,1)}, u32[]{:S(2)}) copy-start(bf16[128,16,256]{2,1,0:T(8,128)(2,1)} %param.27) | copy-start | bytes 3145732
  876.7 296.8 %copy-start.16 = (bf16[128,16,256]{2,1,0:T(8,128)(2,1)S(1)}, bf16[128,16,256]{2,1,0:T(8,128)(2,1)}, u32[]{:S(2)}) copy-start(bf16[128,16,256]{2,1,0:T(8,128)(2,1)} %param.39) | copy-start | bytes 3145732
  (41 other events, 218.9 us)
Sparse Core Ops, SparseCore 0:
  10.2 83.3 all-gather.6
  95.7 78.7 all-gather.12
  176.9 52.5 all-gather.10
  231.9 54.3 all-gather.8
  487.2 239.1 reduce-scatter.4
  728.7 144.4 reduce-scatter.2
  875.8 291.5 all-reduce.4
  1173.8 173.6 all-reduce.6
where the time goes:
time: 1380 us; the launch traced here: 1370 us
  waiting for transfers between devices  816 us (59%)
  matrix products  242 us (18%)
  local copies, waits for them, and re-layouts  165 us (12%)
  other arithmetic  92.5 us (7%)
  blocking collectives  35.8 us (3%)
  between operations  15.2 us (1%)
    psum x1, waiting for transfers between devices, body(): hidden_full = lax.psum(hidden_grad, 'tp')  291 us
    psum x1, waiting for transfers between devices, body(): lax.psum((gain_grad, shift_grad, query_wgrad, key_wgrad, value_wgrad, out...  153 us
    reduce_scatter x1, waiting for transfers between devices, body(): lax.psum_scatter(lax.cond(offset <= last_row, compute, lambda unused: jnp...  141 us
    reduce_scatter x1, waiting for transfers between devices, body(): lax.psum_scatter(branches, 'tp', scatter_dimension=2, tiled=True)  76.5 us
    unnamed x120, local copies, waits for them, and re-layouts  54.2 us
    all_gather x1, waiting for transfers between devices, body(): lax.all_gather(key_rows, 'seq', axis=0, tiled=True)  45.5 us
    all_gather x1, waiting for transfers between devices, body(): lax.all_gather(tokens, 'tp', axis=2, tiled=True)  44.6 us
    dot_general x4, matrix products, raw_scores(): jnp.einsum('qrhd,krhd->rhqk', query_heads, key_heads, preferred_element_t...  43.5 us
  transfers between devices with their start and end apart: 8, of which 8 were waited for; matrix products, arithmetic and copies ran while one was open for 20% of the time, Pallas kernels for 0%

commit v1 on v0

v1 whole, which is shorter than its diff:
```python
from functools import partial

import jax
import jax.numpy as jnp
from jax import lax
from jax.experimental import pallas as pl
from jax.experimental.pallas import tpu as pltpu
from jax.sharding import PartitionSpec as P

DH = 64
ROTARY = 32
PROTEIN_SLOTS = 8
LANES = 128

EPSILON = 1e-05
SCALING = 0.125
NEGATIVE = -1e30
BASE_FREQ = 10000.0
GELU_A = 0.7978845608028654
GELU_B = 0.044715

F32 = jnp.float32
BF16 = jnp.bfloat16
NT = (((1,), (1,)), ((), ()))
TN = (((0,), (0,)), ((), ()))
VMEM_LIMIT = 56 * 1024 * 1024


def behind(kernel, n_in, after, n_scalar=0):
    n_in = n_in + n_scalar

    def wrapped(*refs):
        return kernel(*refs[:n_in], *refs[n_in + len(after) :])

    return wrapped


def work(flops, bytes_accessed, times=3):
    return pl.CostEstimate(flops=times * flops, bytes_accessed=times * bytes_accessed, transcendentals=0)


def unused(after):
    return [pl.BlockSpec(memory_space=pl.ANY)] * len(after)


def params(**more):
    return pltpu.CompilerParams(vmem_limit_bytes=VMEM_LIMIT, **more)


def packing(lengths, extent):
    protein_ends = jnp.cumsum(lengths, axis=1)
    places = jnp.arange(extent, dtype=jnp.int32)
    passed = protein_ends[:, None, :] <= places[None, :, None]
    begins = jnp.max(jnp.where(passed, protein_ends[:, None, :], 0), axis=2)
    padded = places[None, :] >= protein_ends[:, -1:]
    starts = jnp.where(padded, places[None, :], begins)
    return starts, places[None, :] - starts


def turn_tables(inside_position):
    dim_index = jnp.arange(LANES, dtype=jnp.int32) % DH
    halves = (dim_index // 2).astype(F32)
    frequency = jnp.where(dim_index < ROTARY, BASE_FREQ ** (-2.0 * halves / ROTARY), 0.0)
    sign = jnp.where(dim_index % 2 == 0, -1.0, 1.0)
    phase_angle = inside_position.astype(F32)[..., None] * frequency
    return jnp.cos(phase_angle), jnp.sin(phase_angle) * sign


def swap_pairs(x):
    lane = lax.broadcasted_iota(jnp.int32, x.shape, 1)
    return jnp.where(lane % 2 == 0, pltpu.roll(x, LANES - 1, 1), pltpu.roll(x, 1, 1))


def norm_project_kernel(
    x_ref, gain_ref, shift_ref, wq_ref, wk_ref, wv_ref, win_ref, bias_ref, cos_ref, sin_ref,
    hidden_ref, qkv_ref, act_ref, slope_ref, stat_ref,
):
    parts, rows, part = x_ref.shape
    width = parts * part
    embed = wq_ref.shape[1]
    xs = [x_ref[k].astype(F32) for k in range(parts)]
    mean = sum(jnp.sum(x, axis=1, keepdims=True) for x in xs) * (1.0 / width)
    xs = [x - mean for x in xs]
    var = sum(jnp.sum(x * x, axis=1, keepdims=True) for x in xs) * (1.0 / width)
    inverse = lax.rsqrt(var + EPSILON)
    lane = lax.broadcasted_iota(jnp.int32, stat_ref.shape, 1)
    stat_ref[...] = jnp.where(lane == 0, mean, inverse)
    for k in range(parts):
        at = pl.ds(k * part, part)
        hidden_ref[:, at] = (xs[k] * inverse * gain_ref[:, at] + shift_ref[:, at]).astype(BF16)
    hidden = hidden_ref[...]
    cos, sin = cos_ref[...], sin_ref[...]
    for n, w_ref in enumerate((wq_ref, wk_ref)):
        pre = jnp.dot(hidden, w_ref[...], preferred_element_type=F32)
        for g in range(embed // LANES):
            one = pre[:, g * LANES : (g + 1) * LANES]
            qkv_ref[:, pl.ds(n * embed + g * LANES, LANES)] = (
                one * cos + swap_pairs(one) * sin
            ).astype(BF16)
    qkv_ref[:, pl.ds(2 * embed, embed)] = jnp.dot(
        hidden, wv_ref[...], preferred_element_type=F32
    ).astype(BF16)
    v = jnp.dot(hidden, win_ref[...], preferred_element_type=F32) + bias_ref[...]
    square = v * v
    t = jnp.tanh(GELU_A * v * (1.0 + GELU_B * square))
    act_ref[...] = (0.5 * v * (1.0 + t)).astype(BF16)
    slope_ref[...] = 0.5 * (1.0 + t) + 0.5 * v * (1.0 - t * t) * (
        GELU_A * (1.0 + 3.0 * GELU_B * square)
    )


def norm_project(x, gain, shift, wq, wk, wv, win, bias, cos, sin, after=()):
    parts, total, part = x.shape
    width, embed = wq.shape
    inner = win.shape[1]
    rows = min(256, total)
    whole = lambda i: (0, 0)
    block = lambda i: (i, 0)
    return pl.pallas_call(
        behind(norm_project_kernel, 10, after),
        grid=(total // rows,),
        in_specs=[
            pl.BlockSpec((parts, rows, part), lambda i: (0, i, 0)),
            pl.BlockSpec((1, width), whole),
            pl.BlockSpec((1, width), whole),
            pl.BlockSpec((width, embed), whole),
            pl.BlockSpec((width, embed), whole),
            pl.BlockSpec((width, embed), whole),
            pl.BlockSpec((width, inner), whole),
            pl.BlockSpec((1, inner), whole),
            pl.BlockSpec((rows, LANES), block),
            pl.BlockSpec((rows, LANES), block),
            *unused(after),
        ],
        out_specs=[
            pl.BlockSpec((rows, width), block),
            pl.BlockSpec((rows, 3 * embed), block),
            pl.BlockSpec((rows, inner), block),
            pl.BlockSpec((rows, inner), block),
            pl.BlockSpec((rows, LANES), block),
        ],
        out_shape=[
            jax.ShapeDtypeStruct((total, width), BF16),
            jax.ShapeDtypeStruct((total, 3 * embed), BF16),
            jax.ShapeDtypeStruct((total, inner), BF16),
            jax.ShapeDtypeStruct((total, inner), F32),
            jax.ShapeDtypeStruct((total, LANES), F32),
        ],
        compiler_params=params(),
        cost_estimate=work(2 * total * width * (3 * embed + inner), total * (4 * width + 6 * embed + 6 * inner)),
        name="norm_project",
    )(x, gain, shift, wq, wk, wv, win, bias, cos, sin, *after)


def push_back_kernel(c_ref, wo_ref, wout_ref, slope_ref, mixed_grad_ref, inner_grad_ref, bias_ref):
    parts, rows, part = c_ref.shape
    mixed_grad = inner = None
    for k in range(parts):
        at = pl.ds(k * part, part)
        one = jnp.dot(c_ref[k], wo_ref[at, :], preferred_element_type=F32)
        two = jnp.dot(c_ref[k], wout_ref[at, :], preferred_element_type=F32)
        mixed_grad = one if mixed_grad is None else mixed_grad + one
        inner = two if inner is None else inner + two
    mixed_grad_ref[...] = mixed_grad.astype(BF16)
    inner_low = (inner * slope_ref[...]).astype(BF16)
    inner_grad_ref[...] = inner_low

    @pl.when(pl.program_id(0) == 0)
    def _():
        bias_ref[...] = jnp.zeros_like(bias_ref)

    bias_ref[...] += jnp.sum(inner_low.astype(F32), axis=0, keepdims=True)


def push_back(c, wo, wout, slope, after=(), times=3):
    parts, total, part = c.shape
    width, embed = wo.shape
    inner = wout.shape[1]
    rows = min(512, total)
    whole = lambda i: (0, 0)
    block = lambda i: (i, 0)
    return pl.pallas_call(
        behind(push_back_kernel, 4, after),
        grid=(total // rows,),
        in_specs=[
            pl.BlockSpec((parts, rows, part), lambda i: (0, i, 0)),
            pl.BlockSpec((width, embed), whole),
            pl.BlockSpec((width, inner), whole),
            pl.BlockSpec((rows, inner), block),
            *unused(after),
        ],
        out_specs=[
            pl.BlockSpec((rows, embed), block),
            pl.BlockSpec((rows, inner), block),
            pl.BlockSpec((1, inner), whole),
        ],
        out_shape=[
            jax.ShapeDtypeStruct((total, embed), BF16),
            jax.ShapeDtypeStruct((total, inner), BF16),
            jax.ShapeDtypeStruct((1, inner), F32),
        ],
        compiler_params=params(),
        cost_estimate=work(2 * total * width * (embed + inner), total * (2 * width + 2 * embed + 6 * inner), times),
        name="push_back",
    )(c, wo, wout, slope, *after)


def attend_kernel(
    sizes, variant_ref, q_ref, k_ref, v_ref, g_ref, start_ref, cos_ref, sin_ref, out_ref, dk_ref, dv_ref
):
    at = pl.program_id(0)
    span, embed = q_ref.shape
    groups = [pl.ds(n * LANES, LANES) for n in range(embed // LANES)]
    first = lax.broadcasted_iota(jnp.int32, (span, LANES), 1) < DH
    row_at = pl.multiple_of(at * span, span)

    @pl.when(at == 0)
    def _():
        dk_ref[...] = jnp.zeros_like(dk_ref)
        dv_ref[...] = jnp.zeros_like(dv_ref)

    def unturn(x, cos, sin):
        return x * cos - swap_pairs(x) * sin

    def block(count):
        window = count * span
        base = pl.multiple_of(jnp.maximum(at + 1 - count, 0) * span, span)
        keys_at = pl.ds(base, window)
        rows = pl.ds(row_at, span)
        key_place = base + lax.broadcasted_iota(jnp.int32, (span, window), 1)
        query_place = row_at + lax.broadcasted_iota(jnp.int32, (span, window), 0)
        seen = (key_place >= start_ref[...]) & (key_place <= query_place)
        heads = []
        for group in groups:
            q = q_ref[:, group] * jnp.asarray(SCALING, BF16)
            g = g_ref[:, group]
            for mine in (first, jnp.logical_not(first)):
                heads.append((group, jnp.where(mine, q, jnp.zeros_like(q)), jnp.where(mine, g, jnp.zeros_like(g))))
        scores = [
            lax.dot_general(q, k_ref[keys_at, group], NT, preferred_element_type=F32) for group, q, g in heads
        ]
        pushed = [
            lax.dot_general(g, v_ref[keys_at, group], NT, preferred_element_type=F32) for group, q, g in heads
        ]
        weights = []
        for one in scores:
            one = jnp.where(seen, one, NEGATIVE)
            one = jnp.exp(one - jnp.max(one, axis=1, keepdims=True))
            weights.append(one * (1.0 / jnp.sum(one, axis=1, keepdims=True)))
        lows = [one.astype(BF16) for one in weights]
        grads = [
            (one * (push - jnp.sum(one * push, axis=1, keepdims=True))).astype(BF16)
            for one, push in zip(weights, pushed)
        ]
        for n, group in enumerate(groups):
            keys, values = k_ref[keys_at, group], v_ref[keys_at, group]
            pair = (2 * n, 2 * n + 1)
            mixed = [jnp.dot(lows[h], values, preferred_element_type=F32) for h in pair]
            dq = [jnp.dot(grads[h], keys, preferred_element_type=F32) for h in pair]
            dk_ref[keys_at, group] += sum(tn_dot(grads[h], heads[h][1]) for h in pair)
            dv_ref[keys_at, group] += sum(tn_dot(lows[h], heads[h][2]) for h in pair)
            out_ref[rows, group] = jnp.where(first, mixed[0], mixed[1]).astype(BF16)
            turned = jnp.where(first, dq[0], dq[1]) * SCALING
            out_ref[rows, pl.ds(embed + n * LANES, LANES)] = unturn(
                turned, cos_ref[rows, :], sin_ref[rows, :]
            ).astype(BF16)

    for n, count in enumerate(sizes):

        @pl.when(variant_ref[at] == n)
        def _(count=count):
            block(count)

    @pl.when(at == pl.num_programs(0) - 1)
    def _():
        for n, group in enumerate(groups):
            out_ref[:, pl.ds(2 * embed + n * LANES, LANES)] = unturn(
                dk_ref[:, group], cos_ref[...], sin_ref[...]
            ).astype(BF16)
            out_ref[:, pl.ds(3 * embed + n * LANES, LANES)] = dv_ref[:, group].astype(BF16)


def attend(qkv, g, starts, cos, sin, after=()):
    extent, embed = g.shape
    span = min(256, extent)
    spans = extent // span
    sizes = [size for size in range(1, spans) if size <= 4 or size % 2 == 0] + [spans]
    heads = starts.reshape(spans, span)[:, 0]
    need = jnp.arange(spans, dtype=jnp.int32) - heads // span + 1
    variant = jnp.sum((need[:, None] > jnp.asarray(sizes, jnp.int32)[None, :]).astype(jnp.int32), axis=1)
    spec = pl.BlockSpec
    return pl.pallas_call(
        behind(partial(attend_kernel, tuple(sizes)), 7, after, 1),
        grid_spec=pltpu.PrefetchScalarGridSpec(
            num_scalar_prefetch=1,
            grid=(spans,),
            in_specs=[
                spec((span, embed), lambda i, s: (i, 0)),
                spec((extent, embed), lambda i, s: (0, 1)),
                spec((extent, embed), lambda i, s: (0, 2)),
                spec((span, embed), lambda i, s: (i, 0)),
                spec((span, 1), lambda i, s: (i, 0)),
                spec((extent, LANES), lambda i, s: (0, 0)),
                spec((extent, LANES), lambda i, s: (0, 0)),
                *unused(after),
            ],
            out_specs=spec((extent, 4 * embed), lambda i, s: (0, 0)),
            scratch_shapes=[pltpu.VMEM((extent, embed), F32), pltpu.VMEM((extent, embed), F32)],
        ),
        out_shape=jax.ShapeDtypeStruct((extent, 4 * embed), BF16),
        compiler_params=params(),
        cost_estimate=work(12 * embed * extent * extent, extent * embed * 16),
        name="attend",
    )(variant, qkv, qkv, qkv, g, starts[:, None], cos, sin, *after)


def dense_back_kernel(
    back_ref, inner_ref, act_ref, x_ref, stat_ref, gain_ref, wqkv_ref, win_ref, wo_ref, wout_ref,
    out_ref, feature_ref, sums_ref,
):
    parts, rows, part = x_ref.shape
    extra = sums_ref.shape[0]
    total_rows = (out_ref.shape[1] - extra) // 2
    embed = wo_ref.shape[0]
    step = pl.program_id(0)
    mean, inverse = stat_ref[:, 0:1], stat_ref[:, 1:2]

    @pl.when(step == 0)
    def _():
        feature_ref[...] = jnp.zeros_like(feature_ref)
        sums_ref[...] = jnp.zeros_like(sums_ref)

    first = pl.ds(pl.multiple_of(step * rows, rows), rows)
    second = pl.ds(pl.multiple_of(total_rows + step * rows, rows), rows)
    ones = jnp.ones((8, LANES), BF16)
    one = two = None
    for k in range(parts):
        at = pl.ds(k * part, part)
        total = jnp.dot(inner_ref[...], win_ref[:, at], preferred_element_type=F32)
        total += jnp.dot(
            back_ref[:, pl.ds(embed, 3 * embed)], wqkv_ref[:, at], preferred_element_type=F32
        )
        out_ref[k, first, :] = total.astype(BF16)
        out_ref[k, second, :] = (
            jnp.dot(back_ref[:, pl.ds(0, embed)], wo_ref[:, at], preferred_element_type=F32)
            + jnp.dot(act_ref[...], wout_ref[:, at], preferred_element_type=F32)
        ).astype(BF16)
        scaled = (x_ref[k].astype(F32) - mean) * inverse
        product = total * scaled
        feature_ref[0:1, at] += jnp.sum(product, axis=0, keepdims=True)
        feature_ref[1:2, at] += jnp.sum(total, axis=0, keepdims=True)
        gain = gain_ref[:, at]
        for n in range(part // LANES):
            lanes = slice(n * LANES, (n + 1) * LANES)
            gained, moved = total[:, lanes] * gain[:, lanes], product[:, lanes] * gain[:, lanes]
            one = gained if one is None else one + gained
            two = moved if two is None else two + moved
    one, two = (
        lax.dot_general(ones, sums.astype(BF16), NT, preferred_element_type=F32) for sums in (one, two)
    )
    pieces = max(rows // part, 1)
    for start, row in ((0, one), (total_rows // part, two)):
        for n in range(pieces):
            sums_ref[pl.ds(start + step * pieces + n, 1), :] = row[0:1, n * part : (n + 1) * part]

    @pl.when(step == pl.num_programs(0) - 1)
    def _():
        for k in range(parts):
            out_ref[k, pl.ds(2 * total_rows, extra), :] = sums_ref[...].astype(BF16)


def extra_rows(total, part):
    return -(-2 * total // part // 16) * 16


def dense_back(back, inner_grad, act, x, stat, gain, wqkv, win, wo, wout, after=()):
    parts, total, part = x.shape
    embed, width = wo.shape
    inner = win.shape[0]
    rows = min(512, total)
    extra = extra_rows(total, part)
    whole = lambda i: (0, 0)
    block = lambda i: (i, 0)
    return pl.pallas_call(
        behind(dense_back_kernel, 10, after),
        grid=(total // rows,),
        in_specs=[
            pl.BlockSpec((rows, 4 * embed), block),
            pl.BlockSpec((rows, inner), block),
            pl.BlockSpec((rows, inner), block),
            pl.BlockSpec((parts, rows, part), lambda i: (0, i, 0)),
            pl.BlockSpec((rows, LANES), block),
            pl.BlockSpec((1, width), whole),
            pl.BlockSpec((3 * embed, width), whole),
            pl.BlockSpec((inner, width), whole),
            pl.BlockSpec((embed, width), whole),
            pl.BlockSpec((inner, width), whole),
            *unused(after),
        ],
        out_specs=[
            pl.BlockSpec((parts, 2 * total + extra, part), lambda i: (0, 0, 0)),
            pl.BlockSpec((2, width), whole),
        ],
        out_shape=[
            jax.ShapeDtypeStruct((parts, 2 * total + extra, part), BF16),
            jax.ShapeDtypeStruct((2, width), F32),
        ],
        scratch_shapes=[pltpu.VMEM((extra, part), F32)],
        compiler_params=params(),
        cost_estimate=work(2 * total * width * (4 * embed + 2 * inner), total * (6 * width + 8 * embed + 4 * inner)),
        name="dense_back",
    )(back, inner_grad, act, x, stat, gain, wqkv, win, wo, wout, *after)


def tn_dot(left, right):
    return lax.dot_general(left, right, TN, preferred_element_type=F32)


def piece_rows(shapes, devices):
    return [rows * columns // (devices * LANES) for rows, columns in shapes]


def grads_kernel(chunks, steps, n_in, n_total, n_small, carried, last, make, core_ref, *refs):
    at = chunks * n_in
    ins, small_refs, refs = refs[:at], refs[at : at + n_small], refs[at + n_small :]
    earlier, refs = refs[: n_total * carried], refs[n_total * carried :]
    if last:
        keep_ref, send_ref, *totals = refs
    else:
        totals = refs
    at = pl.program_id(0)

    @pl.when(at == 0)
    def _():
        for n, total in enumerate(totals):
            total[...] = earlier[n][...] if carried else jnp.zeros_like(total)

    for c in range(chunks):

        @pl.when(at // steps == c)
        def _(c=c):
            make(ins[c * n_in : (c + 1) * n_in], totals)

    if last:

        @pl.when(at == chunks * steps - 1)
        def _():
            chips = keep_ref.shape[0]
            for core, out_ref in ((core_ref[0], keep_ref), (1 - core_ref[0], send_ref)):
                for chip in range(chips):
                    offset = 0
                    for total in (*totals, *small_refs):
                        rows = total.shape[0] // (2 * chips)
                        start = pl.multiple_of((core * chips + chip) * rows, rows)
                        for n in range(total.shape[1] // LANES):
                            out_ref[chip, pl.ds(offset, rows), :] = total[
                                pl.ds(start, rows), pl.ds(n * LANES, LANES)
                            ].astype(BF16)
                            offset += rows


def feed_make(ins, totals):
    act, hidden, inner_grad, cot = ins
    outer_total, inner_total = totals
    parts, _, part = cot.shape
    left = act[...]
    for k in range(parts):
        outer_total[:, pl.ds(k * part, part)] += tn_dot(left, cot[k])
    inner_total[...] += tn_dot(hidden[...], inner_grad[...])


def head_make(ins, totals):
    back, hidden, cot = ins
    output_total, *projection_totals = totals
    parts, _, part = cot.shape
    embed = output_total.shape[0]
    left = back[:, pl.ds(0, embed)]
    for k in range(parts):
        output_total[:, pl.ds(k * part, part)] += tn_dot(left, cot[k])
    for n, total in enumerate(projection_totals):
        total[...] += tn_dot(hidden[...], back[:, pl.ds((n + 1) * embed, embed)])


def grads(make, shapes, name, core, devices, chunk_arrays, small=(), earlier=(), last=True, after=(), times=3):
    chunks = len(chunk_arrays)
    total = chunk_arrays[0][0].shape[0]
    rows = min(512, total)
    steps = total // rows
    specs, arrays = [], []
    for c, group in enumerate(chunk_arrays):
        pick = lambda i, c=c: jnp.clip(i - c * steps, 0, steps - 1)
        for array in group:
            if array.ndim == 2:
                specs.append(pl.BlockSpec((rows, array.shape[1]), lambda i, s, pick=pick: (pick(i), 0)))
            else:
                specs.append(
                    pl.BlockSpec((array.shape[0], rows, array.shape[2]), lambda i, s, pick=pick: (0, pick(i), 0))
                )
            arrays.append(array)
    for array in (*small, *earlier):
        specs.append(pl.BlockSpec(array.shape, lambda i, s: (0, 0)))
        arrays.append(array)
    packed = (devices // 2, sum(piece_rows((*shapes, *[a.shape for a in small]), devices)), LANES)
    if last:
        out_specs = [pl.BlockSpec(packed, lambda i, s: (0, 0, 0))] * 2
        out_shape = [jax.ShapeDtypeStruct(packed, BF16)] * 2
        scratch_shapes = [pltpu.VMEM(shape, F32) for shape in shapes]
    else:
        out_specs = [pl.BlockSpec(shape, lambda i, s: (0, 0)) for shape in shapes]
        out_shape = [jax.ShapeDtypeStruct(shape, F32) for shape in shapes]
        scratch_shapes = []
    kernel = partial(
        grads_kernel, chunks, steps, len(chunk_arrays[0]), len(shapes), len(small), len(earlier) > 0, last, make
    )
    return pl.pallas_call(
        behind(kernel, len(specs), after, 1),
        grid_spec=pltpu.PrefetchScalarGridSpec(
            num_scalar_prefetch=1,
            grid=(chunks * steps,),
            in_specs=specs + unused(after),
            out_specs=out_specs,
            scratch_shapes=scratch_shapes,
        ),
        out_shape=out_shape,
        compiler_params=params(),
        cost_estimate=work(
            sum(2 * chunks * total * a * b for a, b in shapes), 2 * sum(a.size for a in arrays), times
        ),
        name=name,
    )(core, *arrays, *after)


def fold_kernel(keep_ref, came_ref, out_ref):
    for n in range(keep_ref.shape[0]):
        out_ref[n] = (keep_ref[n].astype(F32) + came_ref[n].astype(F32)).astype(BF16)


def elementwise(kernel, name, arrays, shape=None, after=(), times=3):
    spec = pl.BlockSpec(memory_space=pltpu.VMEM)
    shape = arrays[0].shape if shape is None else shape
    return pl.pallas_call(
        behind(kernel, len(arrays), after),
        in_specs=[spec] * len(arrays) + unused(after),
        out_specs=spec,
        out_shape=jax.ShapeDtypeStruct(shape, BF16),
        compiler_params=params(),
        cost_estimate=work(3 * arrays[0].size, 6 * arrays[0].size, times),
        name=name,
    )(*arrays, *after)


def merge_kernel(pieces_ref, keep_ref, came_ref, out_ref):
    rows = pieces_ref.shape[1]
    total = pieces_ref[0].astype(F32)
    for n in range(1, pieces_ref.shape[0]):
        total += pieces_ref[n].astype(F32)
    total = total.astype(BF16)
    for n in range(out_ref.shape[0]):
        out_ref[n, pl.ds(0, rows), :] = total
        out_ref[n, pl.ds(rows, keep_ref.shape[1]), :] = (
            keep_ref[n].astype(F32) + came_ref[n].astype(F32)
        ).astype(BF16)


def add_kernel(skip, x_ref, out_ref):
    rows = pl.ds(skip, out_ref.shape[1])
    total = x_ref[0, rows, :].astype(F32)
    for n in range(1, x_ref.shape[0]):
        total += x_ref[n, rows, :].astype(F32)
    total = total.astype(BF16)
    for n in range(out_ref.shape[0]):
        out_ref[n] = total


def passed_on(array, after):
    spec = pl.BlockSpec(memory_space=pl.ANY)
    return pl.pallas_call(
        lambda *refs: None,
        in_specs=[spec] * (1 + len(after)),
        out_specs=spec,
        out_shape=jax.ShapeDtypeStruct(array.shape, array.dtype),
        input_output_aliases={0: 0},
        compiler_params=params(),
        name="passed_on",
    )(array, *after)


def unpack_kernel(n_out, core_ref, own_ref, other_ref, *refs):
    matrix_refs, vector_refs, small_refs = refs[:n_out], refs[n_out:], ()
    if len(refs) > n_out:
        vector_refs, small_refs = refs[n_out:-1], refs[-1:]
    chips = own_ref.shape[0]
    for core, ref in ((core_ref[0], own_ref), (1 - core_ref[0], other_ref)):
        for chip in range(chips):
            offset = 0
            for out_ref in (*matrix_refs, *small_refs):
                rows = out_ref.shape[0] // (2 * chips)
                start = pl.multiple_of((core * chips + chip) * rows, rows)
                for block in range(out_ref.shape[1] // LANES):
                    out_ref[pl.ds(start, rows), pl.ds(block * LANES, LANES)] = ref[
                        chip, pl.ds(offset, rows), :
                    ].astype(F32)
                    offset += rows
    row = 0
    for out_ref in vector_refs:
        for block in range(out_ref.shape[1] // LANES):
            out_ref[:, pl.ds(block * LANES, LANES)] = small_refs[0][pl.ds(row, 1), :]
            row += 1


def unpack(core, own, other, shapes, vectors=(), small_shape=None, after=()):
    spec = pl.BlockSpec(memory_space=pltpu.VMEM)
    outs = (*shapes, *[(1, size) for size in vectors])
    return pl.pallas_call(
        behind(partial(unpack_kernel, len(shapes)), 2, after, 1),
        in_specs=[pl.BlockSpec(memory_space=pltpu.SMEM), spec, spec] + unused(after),
        out_specs=[spec] * len(outs),
        out_shape=[jax.ShapeDtypeStruct(shape, F32) for shape in outs],
        scratch_shapes=[pltpu.VMEM(small_shape, F32)] if vectors else [],
        compiler_params=params(),
        cost_estimate=work(own.size, 12 * own.size),
        name="unpack",
    )(core, own, other, *after)


def last_step_kernel(chunks, width, *refs):
    both_refs, stat_refs, tok_refs, cot_refs = (refs[n * chunks : (n + 1) * chunks] for n in range(4))
    gain_ref, bias_ref, out_ref, grad_ref, plain_ref, columns_ref = refs[4 * chunks :]
    per, span, part = tok_refs[0].shape
    halves = part // LANES
    total = per * LANES
    step = pl.program_id(0)

    @pl.when(step == 0)
    def _():
        for c, both_ref in enumerate(both_refs):
            sums = both_ref[pl.ds(2 * total, both_ref.shape[0] - 2 * total), :]
            shape = (sums.shape[0], LANES)
            eye = lax.broadcasted_iota(jnp.int32, shape, 0) == lax.broadcasted_iota(jnp.int32, shape, 1)
            for h in range(halves):
                columns_ref[c * halves + h] = tn_dot(
                    sums[:, h * LANES : (h + 1) * LANES], eye.astype(F32).astype(BF16)
                ) * (1.0 / width)

    here = pl.ds(pl.multiple_of(step * span, span), span)
    for c, (both_ref, stat_ref, tok_ref, cot_ref) in enumerate(zip(both_refs, stat_refs, tok_refs, cot_refs)):
        for n in range(per):
            r = c * per + n
            at = n * LANES + step * span
            hidden_grad = both_ref[pl.ds(pl.multiple_of(at, span), span), :].astype(F32)
            branch = both_ref[pl.ds(pl.multiple_of(total + at, span), span), :].astype(F32)
            columns = columns_ref[c * halves + n % halves, here, :]
            first = columns[:, n // halves : n // halves + 1]
            second = columns[:, (per + n) // halves : (per + n) // halves + 1]
            mean, inverse = stat_ref[n, :, 0:1], stat_ref[n, :, 1:2]
            token = tok_ref[n].astype(F32)
            scaled = (token - mean) * inverse
            plain_ref[:, r, :] = token + branch + bias_ref[...]
            grad_ref[:, r, :] = cot_ref[n].astype(F32) + inverse * (
                hidden_grad * gain_ref[...] - first - scaled * second
            )
    out_ref[...] = plain_ref[...].astype(BF16)


def last_step(boths, stats, tokens, cotangents, gain, bias, width, positions):
    chunks = len(boths)
    total, part = tokens[0].shape
    per = total // positions
    rows = chunks * per
    in_rows = lambda array: array.reshape(per, positions, array.shape[1])
    span = min(32, positions)
    return pl.pallas_call(
        partial(last_step_kernel, chunks, width),
        grid=(positions // span,),
        in_specs=[
            *[pl.BlockSpec(both.shape, lambda i: (0, 0)) for both in boths],
            *[pl.BlockSpec((per, span, LANES), lambda i: (0, i, 0))] * chunks,
            *[pl.BlockSpec((per, span, part), lambda i: (0, i, 0))] * (2 * chunks),
            *[pl.BlockSpec((1, part), lambda i: (0, 0))] * 2,
        ],
        out_specs=[pl.BlockSpec((span, rows, part), lambda i: (i, 0, 0))] * 2,
        out_shape=[
            jax.ShapeDtypeStruct((positions, rows, part), BF16),
            jax.ShapeDtypeStruct((positions, rows, part), F32),
        ],
        scratch_shapes=[
            pltpu.VMEM((span, rows, part), F32),
            pltpu.VMEM((chunks * (part // LANES), LANES, LANES), F32),
        ],
        compiler_params=params(),
        cost_estimate=work(20 * total * part, 12 * total * part),
        name="last_step",
    )(*boths, *map(in_rows, (*stats, *tokens, *cotangents)), gain, bias)


def partner(array, axis, bit):
    size = lax.axis_size(axis)
    return lax.ppermute(array, axis, [(i, i ^ bit) for i in range(size)])


def to_chips(pieces, axis):
    size = lax.axis_size(axis)
    groups = [list(range(core, size, 2)) for core in range(2)]
    return lax.all_to_all(pieces, axis, 0, 0, tiled=True, axis_index_groups=groups)


def small_sum(array, axes):
    for axis in axes:
        bit = 1
        while bit < lax.axis_size(axis):
            array = array + partner(array, axis, bit)
            bit *= 2
    return array


def body(
    tokens, norm_gain, norm_shift, query_weight, key_weight, value_weight, output_weight,
    inner_weight, inner_bias, outer_weight, outer_bias, lengths, cotangent,
):
    shard_len, batch_rows, local_width = tokens.shape
    seq_count, tp_count = lax.axis_size("seq"), lax.axis_size("tp")
    position, width_index = lax.axis_index("seq"), lax.axis_index("tp")
    extent = shard_len * seq_count
    width, embed = query_weight.shape
    inner = inner_weight.shape[1]
    chunks = batch_rows // seq_count

    own_tokens, own_cotangent = (
        [part.reshape(extent, local_width) for part in jnp.split(jnp.swapaxes(array, 0, 1), chunks)]
        for array in (tokens, cotangent)
    )
    back_qkv = jnp.concatenate([w.T for w in (query_weight, key_weight, value_weight)], axis=0)
    back_inner, back_output, back_outer = inner_weight.T, output_weight.T, outer_weight.T
    token_parts = [lax.all_gather(own_tokens[c], "tp") for c in range(chunks)]
    cotangent_parts = [lax.all_gather(own_cotangent[c], "tp") for c in range(chunks)]
    vectors = lax.all_gather(jnp.stack([norm_gain, norm_shift]), "tp", axis=1, tiled=True)
    vectors = vectors.astype(F32)
    gain, shift = vectors[0:1], vectors[1:2]

    starts, places = packing(lengths, extent)
    own_places = lax.dynamic_slice_in_dim(places, position * shard_len, shard_len, 1)
    own_cos, own_sin = turn_tables(own_places.reshape(chunks, extent))
    row_starts = [lax.dynamic_index_in_dim(starts, c * seq_count + position, 0, False) for c in range(chunks)]
    row_places = [lax.dynamic_index_in_dim(places, c * seq_count + position, 0, False) for c in range(chunks)]
    row_tables = [turn_tables(row) for row in row_places]
    bias_row = inner_bias.astype(F32)[None]

    def exchange(array):
        split = array.reshape(seq_count, shard_len, array.shape[-1])
        return lax.all_to_all(split, "seq", 0, 0, tiled=True).reshape(extent, array.shape[-1])

    stages = [dict() for _ in range(chunks)]
    place = jnp.stack([position % 2, position // 2]).astype(jnp.int32)
    feed_shapes = ((inner, width), (width, inner))

    def project(c, after=()):
        o = stages[c]
        o["hidden"], qkv, o["act"], o["slope"], o["stat"] = norm_project(
            token_parts[c], gain, shift, query_weight, key_weight, value_weight, inner_weight,
            bias_row, own_cos[c], own_sin[c], after=after,
        )
        o["qkv_rows"] = exchange(qkv)

    def push(c, after=()):
        o = stages[c]
        mixed_grad, o["inner_grad"], o["bias"] = push_back(
            cotangent_parts[c], back_output, back_outer, o["slope"], after=after, times=20 if c else 3
        )
        o["grad_rows"] = exchange(mixed_grad)

    def feed_grads(c, earlier):
        o = stages[c]
        return tuple(
            grads(
                feed_make, feed_shapes, "feed_grads", place[:1], seq_count,
                [(o["act"], o["hidden"], o["inner_grad"], cotangent_parts[c])],
                earlier=earlier, last=c == chunks - 1,
            )
        )

    def mix(c, after=()):
        o = stages[c]
        o["attention"] = attend(o["qkv_rows"], o["grad_rows"], row_starts[c], *row_tables[c], after=after)
        o["back"] = exchange(o["attention"])

    def finish(c, after=()):
        o = stages[c]
        o["made"], o["feature"] = dense_back(
            o["back"], o["inner_grad"], o["act"], token_parts[c], o["stat"], gain, back_qkv, back_inner,
            output_weight, outer_weight, after=after,
        )
        o["both"] = lax.psum_scatter(o["made"], "tp", scatter_dimension=0)

    feed = ()
    for c in range(chunks):
        if c == 0:
            project(c)
            push(c, after=(stages[c]["qkv_rows"], back_qkv, back_inner))
        else:
            project(c, after=(stages[c - 1]["attention"],))
            finish(c - 1, after=(stages[c]["hidden"],))
            push(c, after=(stages[c - 1]["made"], stages[c]["qkv_rows"]))
        feed = feed_grads(c, feed)
        mix(c, after=feed)
    outs = stages

    def both(make):
        return sum(make(c, outs[c]) for c in range(chunks))

    last = stages[-1]
    feed = elementwise(fold_kernel, "fold", [feed[0], partner(feed[1], "seq", 1)], after=(last["attention"],))
    finish(chunks - 1, after=(feed,))
    feed = to_chips(feed, "seq")

    feature = small_sum(both(lambda c, o: o["feature"]).reshape(-1, LANES), ("tp",)).reshape(2, width)
    feature = lax.dynamic_slice_in_dim(feature, width_index * local_width, local_width, 1)
    small = jnp.concatenate(
        [
            feature.reshape(-1), both(lambda c, o: o["bias"])[0],
            jnp.sum(cotangent.astype(F32), axis=(0, 1)),
        ]
    )
    small_shape = (seq_count * 16, LANES)
    small = jnp.pad(small, (0, small_shape[0] * LANES - small.size)).reshape(small_shape)
    head_shapes = ((embed, width), (width, embed), (width, embed), (width, embed))
    heads = grads(
        head_make, head_shapes, "head_grads", place[:1], seq_count,
        [(o["back"], o["hidden"], cotangent_parts[c]) for c, o in enumerate(stages)],
        small=(small,), after=(last["made"],), times=0,
    )
    merged = elementwise(
        merge_kernel, "merge", [feed, heads[0], partner(heads[1], "seq", 1)],
        (feed.shape[0], feed.shape[1] + heads[0].shape[1], LANES), times=100,
    )
    merged = to_chips(merged, "seq")
    outer_grad, inner_wgrad = unpack(
        place[:1], merged, partner(merged, "seq", 1), feed_shapes, after=tuple(o["both"] for o in stages[:-1])
    )
    heads = elementwise(partial(add_kernel, feed.shape[1]), "add_up", [merged], heads[0].shape)
    heads = to_chips(heads, "seq")

    layer_out, token_grad = last_step(
        [o["both"] for o in outs], [o["stat"] for o in outs], own_tokens, own_cotangent,
        norm_gain.astype(F32)[None], outer_bias.astype(F32)[None], width, shard_len,
    )
    heads = passed_on(heads, (outer_grad, layer_out, token_grad))
    output_grad, query_grad, key_grad, value_grad, *vectors = unpack(
        place[:1], heads, partner(heads, "seq", 1), head_shapes,
        vectors=(local_width, local_width, inner, local_width), small_shape=small_shape,
    )
    gain_grad, shift_grad, inner_bias_grad, outer_bias_grad = (v.reshape(-1) for v in vectors)
    return (
        layer_out, token_grad, gain_grad, shift_grad, query_grad, key_grad, value_grad, output_grad, inner_wgrad,
        inner_bias_grad, outer_grad, outer_bias_grad,
    )


def solution(mesh):
    return jax.shard_map(
        body,
        mesh=mesh,
        in_specs=(
            P("seq", None, "tp"), P("tp"), P("tp"), P(None, "tp"), P(None, "tp"), P(None, "tp"),
            P("tp", None), P(None, "tp"), P("tp"), P("tp", None), P("tp"), P(), P("seq", None, "tp"),
        ),
        out_specs=(
            P("seq", None, "tp"), P("seq", None, "tp"), P("tp"), P("tp"), P(None, "tp"), P(None, "tp"),
            P(None, "tp"), P("tp", None), P(None, "tp"), P("tp"), P("tp", None), P("tp"),
        ),
        check_vma=False,
    )
```

time: 1380 us -> 408 us (0.30)
  waiting for transfers between devices: 816 us -> 97.9 us
  matrix products: 242 us -> 0 us
  Pallas kernels: 0 us -> 155 us
  local copies, waits for them, and re-layouts: 165 us -> 27.7 us
  other arithmetic: 92.5 us -> 14.6 us
  starting transfers between devices: 0.75 us -> 35.4 us
  blocking collectives: 35.8 us -> 54 us
    psum x2 -> x0, waiting for transfers between devices: 444 us -> none  [the longest x1 291 us: body(): hidden_full = lax.psum(hidden_grad, 'tp')]
    dot_general x27 -> x0, matrix products: 242 us -> none  [the longest x4 43.5 us: raw_scores(): jnp.einsum('qrhd,krhd->rhqk', query_heads, key_heads, preferred_element_t...]
    reduce_scatter x2, waiting for transfers between devices: 218 us -> 0.01 us  [finish(): o['both'] = lax.psum_scatter(o['made'], 'tp', scatter_dimension=0)]
    pallas_call x0 -> x18, Pallas kernels: none -> 155 us  [the longest x3 34.1 us: grads(): pl.pallas_call(behind(kernel, len(specs), after, 1), grid_spec=pltpu.Pref...]
    all_gather x4, waiting for transfers between devices: 154 us -> 47.4 us  [the longest x2 31.4 us: body(): token_parts = [lax.all_gather(own_tokens[c], 'tp') for c in range(chunks)]]
    all_to_all x0 -> x1, blocking collectives: none -> 41.3 us  [to_chips(): lax.all_to_all(pieces, axis, 0, 0, tiled=True, axis_index_groups=groups)]
    cond x10 -> x0, local copies, waits for them, and re-layouts: 35.5 us -> none  [the longest x1 31.9 us: body(): lax.cond(offset <= last_row, compute, lambda unused: jnp.zeros((amount, b...]
    all_to_all x0 -> x8, starting transfers between devices: none -> 34.3 us  [the longest x6 26.1 us: exchange(): lax.all_to_all(split, 'seq', 0, 0, tiled=True)]
  transfers between devices with their start and end apart: 8 -> 20, of which waited for: 8 -> 11; matrix products, arithmetic and copies ran while one was open for 20% -> 8% of each run, Pallas kernels for 0% -> 38%
where the time goes in v1:
time: 408 us; the launch traced here: 400 us
  Pallas kernels  155 us (38%)
  waiting for transfers between devices  97.9 us (24%)
  blocking collectives  54 us (13%)
  starting transfers between devices  35.4 us (9%)
  local copies, waits for them, and re-layouts  27.7 us (7%)
  between operations  15 us (4%)
  other arithmetic  14.6 us (4%)
    all_to_all x1, blocking collectives, to_chips(): lax.all_to_all(pieces, axis, 0, 0, tiled=True, axis_index_groups=groups)  41.3 us
    pallas_call x3, Pallas kernels, grads(): pl.pallas_call(behind(kernel, len(specs), after, 1), grid_spec=pltpu.Pref...  34.1 us
    all_to_all x6, waiting for transfers between devices, exchange(): lax.all_to_all(split, 'seq', 0, 0, tiled=True)  31.9 us
    all_gather x2, waiting for transfers between devices, body(): token_parts = [lax.all_gather(own_tokens[c], 'tp') for c in range(chunks)]  31.4 us
    pallas_call x2, Pallas kernels, dense_back(): pl.pallas_call(behind(dense_back_kernel, 10, after), grid=(total // rows,...  27.9 us
    pallas_call x2, Pallas kernels, attend(): pl.pallas_call(behind(partial(attend_kernel, tuple(sizes)), 7, after, 1),...  27 us
    all_to_all x6, starting transfers between devices, exchange(): lax.all_to_all(split, 'seq', 0, 0, tiled=True)  26.1 us
    pallas_call x2, Pallas kernels, norm_project(): pl.pallas_call(behind(norm_project_kernel, 10, after), grid=(total // row...  23.4 us
  transfers between devices with their start and end apart: 20, of which 11 were waited for; matrix products, arithmetic and copies ran while one was open for 8% of the time, Pallas kernels for 38%

profile of v1, /device:TPU:0, one launch (start us, length us, event | category | flops | bytes accessed | tf_op | source)
XLA Modules:
  0.0 399.9 jit_solution(10880049411081917403)
XLA Ops:
  12.7 12.7 %all_gather.16 = bf16[2,1024]{1,0:T(2,128)(2,1)S(1)} all-gather(bf16[2,256]{1,0:T(2,128)(2,1)S(1)} %pad_maximum_fusion.1), channel_id=1, replica_groups=mesh['seq'=8,'tp'=4] {'tp'}, dimensions={1}, use_global_device_ids=true | all-gather | bytes 5120 | tf_op jit(solution)/shard_map/all_gather | solution.py:736
  31.8 27.1 %all-gather.5.cloned.1.call-done.refs_0_.refs_3_ = bf16[4,1024,256]{2,1,0:T(8,128)(2,1)} async-done(((bf16[1,1024,256]{2,1,0:T(8,128)(2,1)}), bf16[4,1024,256]{2,1,0:T(8,128)(2,1)}) %all-gather.5.cloned.1.call-update) | async-done | bytes 2097168 | tf_op jit(solution)/shard_map/all_gather | solution.py:734
  59.0 11.7 %norm_project.2 = (bf16[1024,1024]{1,0:T(8,128)(2,1)}, bf16[1024,768]{1,0:T(8,128)(2,1)}, bf16[1024,1024]{1,0:T(8,128)(2,1)}, f32[1024,1024]{1,0:T(8,128)}, f32[1024,128]{1,0:T(8,128)}) custom-call(bf16[4,1024,256]{2,1,0:T(8,128)(2,1)} %all-gather.5.cloned.1.call-done.refs_0_.refs_3_, f32[1,1024]{1,0:T(1,128)} %get-tuple-element.113.refs_1_.refs_5_, ...), custom_call_target="tpu_custom_call" | custom-call | flops 11274289152 | bytes 36175872 | tf_op jit(solution)/shard_map/norm_project/pallas_call | solution.py:119
  90.4 5.6 %fusion.2 = (f32[1024,128]{1,0:T(8,128)}, f32[1024,128]{1,0:T(8,128)}, f32[1024,128]{1,0:T(8,128)}, f32[1024,128]{1,0:T(8,128)}) fusion(f32[1024]{0:T(1024)S(1)} %bitcast.94, f32[128]{0:T(128)S(1)} %get-tuple-element.118, f32[128]{0:T(128)S(1)} %get-tuple-element.119, f32[1024]{0:T(1024)S(1)} %bitcast.95), kind=kLoop, calls=%fused_computation.12 | loop fusion | flops 524288 | bytes 2106368 | tf_op jit(solution)/shard_map/mul | solution.py:66
  96.0 9.3 %all-gather.7.cloned.1.call-done.refs_0_.refs_4_.refs_3_ = bf16[4,1024,256]{2,1,0:T(8,128)(2,1)} async-done(((bf16[1,1024,256]{2,1,0:T(8,128)(2,1)}), bf16[4,1024,256]{2,1,0:T(8,128)(2,1)}) %all-gather.7.cloned.1.call-update) | async-done | bytes 2097168 | tf_op jit(solution)/shard_map/all_gather | solution.py:735
  105.2 7.1 %push_back.2 = (bf16[1024,256]{1,0:T(8,128)(2,1)}, bf16[1024,1024]{1,0:T(8,128)(2,1)}, f32[1,1024]{1,0:T(1,128)}) custom-call(bf16[4,1024,256]{2,1,0:T(8,128)(2,1)} %all-gather.7.cloned.1.call-done.refs_0_.refs_4_.refs_3_, bf16[1024,256]{1,0:T(8,128)(2,1)} %bitcast.88, bf16[1024,1024]{1,0:T(8,128)(2,1)} %bitcast.77, f32[1024,1024]{1,0:T(8,128)} %get-tuple-element.51.refs_3_, ...), custom_call_target="tpu_custom_call" | custom-call | flops 8053063680 | bytes 26738688 | tf_op jit(solution)/shard_map/push_back/pallas_call | solution.py:182
  116.0 10.9 %feed_grads.2 = (f32[1024,1024]{1,0:T(8,128)}, f32[1024,1024]{1,0:T(8,128)}) custom-call(s32[1]{0:T(128)} %bitcast.20.refs_0_, bf16[1024,1024]{1,0:T(8,128)(2,1)} %get-tuple-element.53.refs_1_.refs_2_, bf16[1024,1024]{1,0:T(8,128)(2,1)} %get-tuple-element.54.refs_2_, bf16[1024,1024]{1,0:T(8,128)(2,1)} %get-tuple-element.55.refs_3_.refs_1_, ...), custom_call_target="tpu_custom_call" | custom-call | flops 12884901888 | bytes 25165824 | tf_op jit(solution)/shard_map/feed_grads/pallas_call | solution.py:515
  127.7 14.1 %attend.2.refs_10_ = bf16[1024,1024]{1,0:T(8,128)(2,1)} custom-call(s32[4]{0:T(128)} %get-tuple-element.91.refs_0_, bf16[1024,768]{1,0:T(8,128)(2,1)} %bitcast.7.refs_4_.refs_1_.refs_2_.refs_3_, bf16[1024,768]{1,0:T(8,128)(2,1)} %bitcast.7.refs_4_.refs_1_.refs_2_.refs_3_, bf16[1024,768]{1,0:T(8,128)(2,1)} %bitcast.7.refs_4_.refs_1_.refs_2_.refs_3_, ...), custom_call_target="tpu_custom_call" | custom-call | flops 9663676416 | bytes 12582912 | tf_op jit(solution)/shard_map/attend/pallas_call | solution.py:292
  152.1 11.7 %norm_project.3 = (bf16[1024,1024]{1,0:T(8,128)(2,1)}, bf16[1024,768]{1,0:T(8,128)(2,1)}, bf16[1024,1024]{1,0:T(8,128)(2,1)}, f32[1024,1024]{1,0:T(8,128)}, f32[1024,128]{1,0:T(8,128)}) custom-call(bf16[4,1024,256]{2,1,0:T(8,128)(2,1)} %all-gather.9.cloned.1.call-done.refs_0_.refs_3_, f32[1,1024]{1,0:T(1,128)} %get-tuple-element.113.refs_1_.refs_5_, ...), custom_call_target="tpu_custom_call" | custom-call | flops 11274289152 | bytes 36175872 | tf_op jit(solution)/shard_map/norm_project/pallas_call | solution.py:119
  163.8 9.1 %all-to-all-done.2 = bf16[8,128,1024]{2,1,0:T(8,128)(2,1)S(1)} async-done(((bf16[8,128,1024]{2,1,0:T(8,128)(2,1)}), bf16[8,128,1024]{2,1,0:T(8,128)(2,1)S(1)}, u32[]{:S(2)}, u32[]{:S(2)}) %all-to-all-start.2) | async-done | bytes 2097184 | tf_op jit(solution)/shard_map/all_to_all | solution.py:750
  177.2 14.0 %dense_back.2 = (bf16[4,2064,256]{2,1,0:T(8,128)(2,1)}, f32[2,1024]{1,0:T(2,128)}) custom-call(bf16[1024,1024]{1,0:T(8,128)(2,1)} %bitcast.61, bf16[1024,1024]{1,0:T(8,128)(2,1)} %get-tuple-element.55.refs_3_.refs_1_, bf16[1024,1024]{1,0:T(8,128)(2,1)} %get-tuple-element.53.refs_1_.refs_2_, ...), custom_call_target="tpu_custom_call" | custom-call | flops 19327352832 | bytes 37748736 | tf_op jit(solution)/shard_map/dense_back/pallas_call | solution.py:384
  191.2 6.7 %all-gather.11.cloned.1.call-done.refs_0_.refs_4_.refs_6_ = bf16[4,1024,256]{2,1,0:T(8,128)(2,1)} async-done(((bf16[1,1024,256]{2,1,0:T(8,128)(2,1)}), bf16[4,1024,256]{2,1,0:T(8,128)(2,1)}) %all-gather.11.cloned.1.call-update) | async-done | bytes 2097168 | tf_op jit(solution)/shard_map/all_gather | solution.py:735
  198.2 7.0 %push_back.3 = (bf16[1024,256]{1,0:T(8,128)(2,1)}, bf16[1024,1024]{1,0:T(8,128)(2,1)}, f32[1,1024]{1,0:T(1,128)}) custom-call(bf16[4,1024,256]{2,1,0:T(8,128)(2,1)} %all-gather.11.cloned.1.call-done.refs_0_.refs_4_.refs_6_, bf16[1024,256]{1,0:T(8,128)(2,1)} %bitcast.89, bf16[1024,1024]{1,0:T(8,128)(2,1)} %bitcast.78, ...), custom_call_target="tpu_custom_call" | custom-call | flops 53687091200 | bytes 178257920 | tf_op jit(solution)/shard_map/push_back/pallas_call | solution.py:182
  208.8 12.5 %feed_grads.3 = (bf16[4,2048,128]{2,1,0:T(8,128)(2,1)}, bf16[4,2048,128]{2,1,0:T(8,128)(2,1)}) custom-call(s32[1]{0:T(128)} %bitcast.20.refs_0_, bf16[1024,1024]{1,0:T(8,128)(2,1)} %get-tuple-element.64.refs_1_.refs_2_, bf16[1024,1024]{1,0:T(8,128)(2,1)} %get-tuple-element.59.refs_10_.refs_2_.refs_5_, bf16[1024,1024]{1,0:T(8,128)(2,1)} %get-tuple-element.65.refs_3_.refs_1_, ...), custom_call_target="tpu_custom_call" | custom-call | flops 12884901888 | bytes 37748736 | tf_op jit(solution)/shard_map/feed_grads/pallas_call | solution.py:515
  222.5 12.9 %attend.3.refs_2_ = bf16[1024,1024]{1,0:T(8,128)(2,1)} custom-call(s32[4]{0:T(128)} %get-tuple-element.90.refs_0_, bf16[1024,768]{1,0:T(8,128)(2,1)} %bitcast.28.refs_5_.refs_1_.refs_2_.refs_3_, bf16[1024,768]{1,0:T(8,128)(2,1)} %bitcast.28.refs_5_.refs_1_.refs_2_.refs_3_, bf16[1024,768]{1,0:T(8,128)(2,1)} %bitcast.28.refs_5_.refs_1_.refs_2_.refs_3_, ...), custom_call_target="tpu_custom_call" | custom-call | flops 9663676416 | bytes 12582912 | tf_op jit(solution)/shard_map/attend/pallas_call | solution.py:292
  235.5 5.8 %all-to-all-start.5 = ((bf16[8,128,1024]{2,1,0:T(8,128)(2,1)}), bf16[8,128,1024]{2,1,0:T(8,128)(2,1)S(1)}, u32[]{:S(2)}, u32[]{:S(2)}) async-start(bf16[8,128,1024]{2,1,0:T(8,128)(2,1)} %bitcast.65), calls=%async_computation.6 | async-start | bytes 4194304 | tf_op jit(solution)/shard_map/all_to_all | solution.py:750
  245.3 22.6 %all-to-all-done.5 = bf16[8,128,1024]{2,1,0:T(8,128)(2,1)S(1)} async-done(((bf16[8,128,1024]{2,1,0:T(8,128)(2,1)}), bf16[8,128,1024]{2,1,0:T(8,128)(2,1)S(1)}, u32[]{:S(2)}, u32[]{:S(2)}) %all-to-all-start.5) | async-done | bytes 2097184 | tf_op jit(solution)/shard_map/all_to_all | solution.py:750
  269.2 14.0 %dense_back.3 = (bf16[4,2064,256]{2,1,0:T(8,128)(2,1)}, f32[2,1024]{1,0:T(2,128)}) custom-call(bf16[1024,1024]{1,0:T(8,128)(2,1)} %bitcast.63, bf16[1024,1024]{1,0:T(8,128)(2,1)} %get-tuple-element.65.refs_3_.refs_1_, bf16[1024,1024]{1,0:T(8,128)(2,1)} %get-tuple-element.64.refs_1_.refs_2_, ...), custom_call_target="tpu_custom_call" | custom-call | flops 19327352832 | bytes 37748736 | tf_op jit(solution)/shard_map/dense_back/pallas_call | solution.py:384
  287.2 6.3 %collective-permute-done.1 = f32[16,128]{1,0:T(8,128)S(1)} collective-permute-done((f32[16,128]{1,0:T(8,128)S(1)}, f32[16,128]{1,0:T(8,128)S(1)}, u32[]{:S(2)}, u32[]{:S(2)}) %collective-permute-start.1) | collective-permute-done | bytes 8224 | tf_op jit(solution)/shard_map/ppermute | solution.py:698
  293.9 5.5 %collective-permute-done.2 = f32[16,128]{1,0:T(8,128)S(1)} collective-permute-done((f32[16,128]{1,0:T(8,128)S(1)}, f32[16,128]{1,0:T(8,128)S(1)}, u32[]{:S(2)}, u32[]{:S(2)}) %collective-permute-start.2) | collective-permute-done | bytes 8224 | tf_op jit(solution)/shard_map/ppermute | solution.py:698
  300.1 10.7 %head_grads.1 = (bf16[4,1040,128]{2,1,0:T(8,128)(2,1)}, bf16[4,1040,128]{2,1,0:T(8,128)(2,1)}) custom-call(s32[1]{0:T(128)} %bitcast.20.refs_0_, bf16[1024,1024]{1,0:T(8,128)(2,1)} %bitcast.62, bf16[1024,1024]{1,0:T(8,128)(2,1)} %get-tuple-element.54.refs_2_, bf16[4,1024,256]{2,1,0:T(8,128)(2,1)} %all-gather.7.cloned.1.call-done.refs_0_.refs_4_.refs_3_, ...), custom_call_target="tpu_custom_call" | custom-call | tf_op jit(solution)/shard_map/head_grads/pallas_call | solution.py:515
  319.7 41.3 %all_to_all.45.refs_0_.refs_1_ = bf16[4,3088,128]{2,1,0:T(8,128)(2,1)S(1)} all-to-all(bf16[4,3088,128]{2,1,0:T(8,128)(2,1)} %merge.1), channel_id=1, replica_groups={{0,8,16,24},{4,12,20,28},{1,9,17,25},{5,13,21,29},{2,10,18,26},{6,14,22..., dimensions={0} | all-to-all | bytes 6324224 | tf_op jit(solution)/shard_map/all_to_all | solution.py:704
  371.3 7.0 %unpack.2 = (f32[1024,1024]{1,0:T(8,128)}, f32[1024,1024]{1,0:T(8,128)}) custom-call(s32[1]{0:T(128)} %bitcast.20.refs_0_, bf16[4,3088,128]{2,1,0:T(8,128)(2,1)} %copy-done, bf16[4,3088,128]{2,1,0:T(8,128)(2,1)} %collective-permute-done.4.refs_2_, bf16[2064,256]{1,0:T(8,128)(2,1)} %bitcast.70), custom_call_target="tpu_custom_call" | custom-call | flops 4743168 | bytes 56918016 | tf_op jit(solution)/shard_map/unpack/pallas_call | solution.py:614
  378.3 6.7 %last_step.1 = (bf16[128,16,256]{2,1,0:T(8,128)(2,1)}, f32[128,16,256]{2,1,0:T(8,128)}) custom-call(bf16[2064,256]{1,0:T(8,128)(2,1)} %bitcast.71, bf16[2064,256]{1,0:T(8,128)(2,1)} %bitcast.85, f32[8,128,128]{2,1,0:T(8,128)} %bitcast.86, f32[8,128,128]{2,1,0:T(8,128)} %bitcast.87, bf16[8,128,256]{2,1,0:T(8,128)(2,1)} %get-tuple-element.101.refs_4_, ...), custom_call_target="tpu_custom_call" | custom-call | flops 15728640 | bytes 9437184 | tf_op jit(solution)/shard_map/last_step/pallas_call | solution.py:672
  (140 shorter events, 92.7 us)
Async XLA Ops:
  7.2 51.8 %all-gather.5.cloned.1.call-start = ((), (), s32[]{:S(2)}) async-start(), calls=%async_computation.11 | async-start | bytes 2621440 | tf_op jit(solution)/shard_map/all_gather | solution.py:734
  10.0 95.2 %all-gather.7.cloned.1.call-start = ((), (), s32[]{:S(2)}) async-start(), calls=%async_computation.12 | async-start | bytes 2621440 | tf_op jit(solution)/shard_map/all_gather | solution.py:735
  70.6 34.6 %all-to-all-start = ((bf16[8,128,768]{2,1,0:T(8,128)(2,1)}), bf16[8,128,768]{2,1,0:T(8,128)(2,1)}, u32[]{:S(2)}, u32[]{:S(2)}) async-start(bf16[8,128,768]{2,1,0:T(8,128)(2,1)} %bitcast.83), calls=%async_computation | async-start | bytes 3145728 | tf_op jit(solution)/shard_map/all_to_all | solution.py:750
  75.1 77.0 %all-gather.9.cloned.1.call-start = ((), (), s32[]{:S(2)}) async-start(), calls=%async_computation.13 | async-start | bytes 2621440 | tf_op jit(solution)/shard_map/all_gather | solution.py:734
  82.0 7.1 %copy-start.7 = (bf16[1024,256]{0,1:T(8,128)(2,1)S(1)}, bf16[1024,256]{0,1:T(8,128)(2,1)}, u32[]{:S(2)}) copy-start(bf16[1024,256]{0,1:T(8,128)(2,1)} %copy.77) | copy-start | bytes 1572868
  112.3 14.6 %all-to-all-start.1 = ((bf16[8,128,256]{2,1,0:T(8,128)(2,1)}), bf16[8,128,256]{2,1,0:T(8,128)(2,1)S(1)}, u32[]{:S(2)}, u32[]{:S(2)}) async-start(bf16[8,128,256]{2,1,0:T(8,128)(2,1)} %bitcast.93), calls=%async_computation.1 | async-start | bytes 1048576 | tf_op jit(solution)/shard_map/all_to_all | solution.py:750
  141.8 31.1 %all-to-all-start.2 = ((bf16[8,128,1024]{2,1,0:T(8,128)(2,1)}), bf16[8,128,1024]{2,1,0:T(8,128)(2,1)S(1)}, u32[]{:S(2)}, u32[]{:S(2)}) async-start(bf16[8,128,1024]{2,1,0:T(8,128)(2,1)} %bitcast.79), calls=%async_computation.2 | async-start | bytes 4194304 | tf_op jit(solution)/shard_map/all_to_all | solution.py:750
  146.2 51.7 %all-gather.11.cloned.1.call-start = ((), (), s32[]{:S(2)}) async-start(), calls=%async_computation.15 | async-start | bytes 2621440 | tf_op jit(solution)/shard_map/all_gather | solution.py:735
  172.9 25.3 %all-to-all-start.3 = ((bf16[8,128,768]{2,1,0:T(8,128)(2,1)}), bf16[8,128,768]{2,1,0:T(8,128)(2,1)}, u32[]{:S(2)}, u32[]{:S(2)}) async-start(bf16[8,128,768]{2,1,0:T(8,128)(2,1)} %bitcast.84), calls=%async_computation.4 | async-start | bytes 3145728 | tf_op jit(solution)/shard_map/all_to_all | solution.py:750
  177.2 194.1 %reduce-scatter.3.cloned.1.call-start = ((), (), s32[]{:S(2)}) async-start(), calls=%async_computation.14 | async-start | bytes 5283840 | tf_op jit(solution)/shard_map/reduce_scatter | solution.py:792
  205.2 16.5 %all-to-all-start.4 = ((bf16[8,128,256]{2,1,0:T(8,128)(2,1)}), bf16[8,128,256]{2,1,0:T(8,128)(2,1)S(1)}, u32[]{:S(2)}, u32[]{:S(2)}) async-start(bf16[8,128,256]{2,1,0:T(8,128)(2,1)} %bitcast.91), calls=%async_computation.5 | async-start | bytes 1048576 | tf_op jit(solution)/shard_map/all_to_all | solution.py:750
  221.2 20.0 %collective-permute-start = (bf16[4,2048,128]{2,1,0:T(8,128)(2,1)}, bf16[4,2048,128]{2,1,0:T(8,128)(2,1)}, u32[]{:S(2)}, u32[]{:S(2)}) collective-permute-start(bf16[4,2048,128]{2,1,0:T(8,128)(2,1)} %get-tuple-element.67.refs_9_), channel_id=1, source_target_pairs={{0,4},{4,0},{8,12},{12,8},{16,20},{20,16},{24,28},{28,24},{1,5},{5... | collective-permute-start | bytes 6291464 | tf_op jit(solution)/shard_map/ppermute | solution.py:698
  235.5 32.4 %all-to-all-start.5 = ((bf16[8,128,1024]{2,1,0:T(8,128)(2,1)}), bf16[8,128,1024]{2,1,0:T(8,128)(2,1)S(1)}, u32[]{:S(2)}, u32[]{:S(2)}) async-start(bf16[8,128,1024]{2,1,0:T(8,128)(2,1)} %bitcast.65), calls=%async_computation.6 | async-start | bytes 4194304 | tf_op jit(solution)/shard_map/all_to_all | solution.py:750
  241.2 137.1 %reduce-scatter.5.cloned.1.call-start = ((), (), s32[]{:S(2)}) async-start(), calls=%async_computation.16 | async-start | bytes 5283840 | tf_op jit(solution)/shard_map/reduce_scatter | solution.py:792
  283.3 10.3 %copy-start.5 = (bf16[128,16,256]{2,1,0:T(8,128)(2,1)S(1)}, bf16[128,16,256]{2,1,0:T(8,128)(2,1)}, u32[]{:S(2)}) copy-start(bf16[128,16,256]{2,1,0:T(8,128)(2,1)} %param.27) | copy-start | bytes 3145732
  283.3 10.6 %copy-start.16 = (f32[1,1024]{1,0:T(1,128)S(1)}, f32[1,1024]{1,0:T(1,128)}, u32[]{:S(2)}) copy-start(f32[1,1024]{1,0:T(1,128)} %get-tuple-element.74) | copy-start | bytes 12292
  283.3 10.6 %copy-start.17 = (f32[1,1024]{1,0:T(1,128)S(1)}, f32[1,1024]{1,0:T(1,128)}, u32[]{:S(2)}) copy-start(f32[1,1024]{1,0:T(1,128)} %get-tuple-element.75) | copy-start | bytes 12292
  283.3 30.4 %all-to-all-start.6 = ((bf16[4,2048,128]{2,1,0:T(8,128)(2,1)}), bf16[4,2048,128]{2,1,0:T(8,128)(2,1)S(1)}, u32[]{:S(2)}, u32[]{:S(2)}) async-start(bf16[4,2048,128]{2,1,0:T(8,128)(2,1)} %fold.1.refs_10_), calls=%async_computation.8 | async-start | bytes 4194304 | tf_op jit(solution)/shard_map/all_to_all | solution.py:704
  287.2 6.4 %collective-permute-start.1 = (f32[16,128]{1,0:T(8,128)S(1)}, f32[16,128]{1,0:T(8,128)S(1)}, u32[]{:S(2)}, u32[]{:S(2)}) collective-permute-start(f32[16,128]{1,0:T(8,128)S(1)} %reshape.228), channel_id=1, source_target_pairs={{0,1},{1,0},{2,3},{3,2},{4,5},{5,4},{6,7},{7,6},{8,9},{9,8},{10,11... | collective-permute-start | bytes 24584 | tf_op jit(solution)/shard_map/ppermute | solution.py:698
  293.5 5.8 %collective-permute-start.2 = (f32[16,128]{1,0:T(8,128)S(1)}, f32[16,128]{1,0:T(8,128)S(1)}, u32[]{:S(2)}, u32[]{:S(2)}) collective-permute-start(f32[16,128]{1,0:T(8,128)S(1)} %add.128), channel_id=1, source_target_pairs={{0,2},{1,3},{2,0},{3,1},{4,6},{5,7},{6,4},{7,5},{8,10},{9,11},{10,... | collective-permute-start | bytes 24584 | tf_op jit(solution)/shard_map/ppermute | solution.py:698
  310.7 2.9 collective-permute-start.3
  361.0 10.2 %collective-permute-start.4 = (bf16[4,3088,128]{2,1,0:T(8,128)(2,1)S(1)}, bf16[4,3088,128]{2,1,0:T(8,128)(2,1)}, u32[]{:S(2)}, u32[]{:S(2)}) collective-permute-start(bf16[4,3088,128]{2,1,0:T(8,128)(2,1)S(1)} %all_to_all.45.refs_0_.refs_1_), channel_id=1, source_target_pairs={{0,4},{4,0},{8,12},{12,8},{16,20},{20,16},{24,28},{28,24},{1,5},{5... | collective-permute-start | bytes 9486344 | tf_op jit(solution)/shard_map/ppermute | solution.py:698
  365.7 19.3 %all-to-all-start.8 = ((bf16[4,1040,128]{2,1,0:T(8,128)(2,1)}), bf16[4,1040,128]{2,1,0:T(8,128)(2,1)}, u32[]{:S(2)}, u32[]{:S(2)}) async-start(bf16[4,1040,128]{2,1,0:T(8,128)(2,1)} %add_up.1), calls=%async_computation.10 | async-start | bytes 2129920 | tf_op jit(solution)/shard_map/all_to_all | solution.py:704
  385.0 3.0 collective-permute-start.5
  (21 other events, 60.5 us)
Sparse Core Ops, SparseCore 0:
  10.2 48.7 all-gather.4
  60.5 44.6 all-gather.6
  107.4 44.6 all-gather.8
  153.5 44.4 all-gather.10
  200.1 76.0 reduce-scatter.2
  283.3 74.5 reduce-scatter.4

commit v2 on v1

--- a/solution.py
+++ b/solution.py
@@ -420,20 +420,16 @@
     return [rows * columns // (devices * LANES) for rows, columns in shapes]
 
 
-def grads_kernel(chunks, steps, n_in, n_total, n_small, carried, last, make, core_ref, *refs):
+def grads_kernel(chunks, steps, n_in, n_small, make, core_ref, *refs):
     at = chunks * n_in
     ins, small_refs, refs = refs[:at], refs[at : at + n_small], refs[at + n_small :]
-    earlier, refs = refs[: n_total * carried], refs[n_total * carried :]
-    if last:
-        keep_ref, send_ref, *totals = refs
-    else:
-        totals = refs
+    keep_ref, send_ref, *totals = refs
     at = pl.program_id(0)
 
     @pl.when(at == 0)
     def _():
-        for n, total in enumerate(totals):
-            total[...] = earlier[n][...] if carried else jnp.zeros_like(total)
+        for total in totals:
+            total[...] = jnp.zeros_like(total)
 
     for c in range(chunks):
 
@@ -441,22 +437,20 @@
         def _(c=c):
             make(ins[c * n_in : (c + 1) * n_in], totals)
 
-    if last:
-
-        @pl.when(at == chunks * steps - 1)
-        def _():
-            chips = keep_ref.shape[0]
-            for core, out_ref in ((core_ref[0], keep_ref), (1 - core_ref[0], send_ref)):
-                for chip in range(chips):
-                    offset = 0
-                    for total in (*totals, *small_refs):
-                        rows = total.shape[0] // (2 * chips)
-                        start = pl.multiple_of((core * chips + chip) * rows, rows)
-                        for n in range(total.shape[1] // LANES):
-                            out_ref[chip, pl.ds(offset, rows), :] = total[
-                                pl.ds(start, rows), pl.ds(n * LANES, LANES)
-                            ].astype(BF16)
-                            offset += rows
+    @pl.when(at == chunks * steps - 1)
+    def _():
+        chips = keep_ref.shape[0]
+        for core, out_ref in ((core_ref[0], keep_ref), (1 - core_ref[0], send_ref)):
+            for chip in range(chips):
+                offset = 0
+                for total in (*totals, *small_refs):
+                    rows = total.shape[0] // (2 * chips)
+                    start = pl.multiple_of((core * chips + chip) * rows, rows)
+                    for n in range(total.shape[1] // LANES):
+                        out_ref[chip, pl.ds(offset, rows), :] = total[
+                            pl.ds(start, rows), pl.ds(n * LANES, LANES)
+                        ].astype(BF16)
+                        offset += rows
 
 
 def feed_make(ins, totals):
@@ -481,7 +475,7 @@
         total[...] += tn_dot(hidden[...], back[:, pl.ds((n + 1) * embed, embed)])
 
 
-def grads(make, shapes, name, core, devices, chunk_arrays, small=(), earlier=(), last=True, after=(), times=3):
+def grads(make, shapes, name, core, devices, chunk_arrays, small=(), after=(), times=3):
     chunks = len(chunk_arrays)
     total = chunk_arrays[0][0].shape[0]
     rows = min(512, total)
@@ -497,31 +491,21 @@
                     pl.BlockSpec((array.shape[0], rows, array.shape[2]), lambda i, s, pick=pick: (0, pick(i), 0))
                 )
             arrays.append(array)
-    for array in (*small, *earlier):
+    for array in small:
         specs.append(pl.BlockSpec(array.shape, lambda i, s: (0, 0)))
         arrays.append(array)
     packed = (devices // 2, sum(piece_rows((*shapes, *[a.shape for a in small]), devices)), LANES)
-    if last:
-        out_specs = [pl.BlockSpec(packed, lambda i, s: (0, 0, 0))] * 2
-        out_shape = [jax.ShapeDtypeStruct(packed, BF16)] * 2
-        scratch_shapes = [pltpu.VMEM(shape, F32) for shape in shapes]
-    else:
-        out_specs = [pl.BlockSpec(shape, lambda i, s: (0, 0)) for shape in shapes]
-        out_shape = [jax.ShapeDtypeStruct(shape, F32) for shape in shapes]
-        scratch_shapes = []
-    kernel = partial(
-        grads_kernel, chunks, steps, len(chunk_arrays[0]), len(shapes), len(small), len(earlier) > 0, last, make
-    )
+    kernel = partial(grads_kernel, chunks, steps, len(chunk_arrays[0]), len(small), make)
     return pl.pallas_call(
         behind(kernel, len(specs), after, 1),
         grid_spec=pltpu.PrefetchScalarGridSpec(
             num_scalar_prefetch=1,
             grid=(chunks * steps,),
             in_specs=specs + unused(after),
-            out_specs=out_specs,
-            scratch_shapes=scratch_shapes,
+            out_specs=[pl.BlockSpec(packed, lambda i, s: (0, 0, 0))] * 2,
+            scratch_shapes=[pltpu.VMEM(shape, F32) for shape in shapes],
         ),
-        out_shape=out_shape,
+        out_shape=[jax.ShapeDtypeStruct(packed, BF16)] * 2,
         compiler_params=params(),
         cost_estimate=work(
             sum(2 * chunks * total * a * b for a, b in shapes), 2 * sum(a.size for a in arrays), times
@@ -530,12 +514,12 @@
     )(core, *arrays, *after)
 
 
-def fold_kernel(keep_ref, came_ref, out_ref):
-    for n in range(keep_ref.shape[0]):
-        out_ref[n] = (keep_ref[n].astype(F32) + came_ref[n].astype(F32)).astype(BF16)
-
-
-def elementwise(kernel, name, arrays, shape=None, after=(), times=3):
+def fold_kernel(*refs):
+    for n in range(refs[-1].shape[0]):
+        refs[-1][n] = sum(ref[n].astype(F32) for ref in refs[:-1]).astype(BF16)
+
+
+def elementwise(kernel, name, arrays, shape=None, after=()):
     spec = pl.BlockSpec(memory_space=pltpu.VMEM)
     shape = arrays[0].shape if shape is None else shape
     return pl.pallas_call(
@@ -544,7 +528,7 @@
         out_specs=spec,
         out_shape=jax.ShapeDtypeStruct(shape, BF16),
         compiler_params=params(),
-        cost_estimate=work(3 * arrays[0].size, 6 * arrays[0].size, times),
+        cost_estimate=work(3 * arrays[0].size, 6 * arrays[0].size),
         name=name,
     )(*arrays, *after)
 
@@ -768,15 +752,13 @@
         )
         o["grad_rows"] = exchange(mixed_grad)
 
-    def feed_grads(c, earlier):
+    def feed_grads(c):
         o = stages[c]
-        return tuple(
-            grads(
-                feed_make, feed_shapes, "feed_grads", place[:1], seq_count,
-                [(o["act"], o["hidden"], o["inner_grad"], cotangent_parts[c])],
-                earlier=earlier, last=c == chunks - 1,
-            )
+        keep, send = grads(
+            feed_make, feed_shapes, "feed_grads", place[:1], seq_count,
+            [(o["act"], o["hidden"], o["inner_grad"], cotangent_parts[c])],
         )
+        return keep, partner(send, "seq", 1)
 
     def mix(c, after=()):
         o = stages[c]
@@ -791,7 +773,7 @@
         )
         o["both"] = lax.psum_scatter(o["made"], "tp", scatter_dimension=0)
 
-    feed = ()
+    feed = []
     for c in range(chunks):
         if c == 0:
             project(c)
@@ -800,15 +782,15 @@
             project(c, after=(stages[c - 1]["attention"],))
             finish(c - 1, after=(stages[c]["hidden"],))
             push(c, after=(stages[c - 1]["made"], stages[c]["qkv_rows"]))
-        feed = feed_grads(c, feed)
-        mix(c, after=feed)
+        feed.extend(feed_grads(c))
+        mix(c, after=(feed[-2],))
     outs = stages
 
     def both(make):
         return sum(make(c, outs[c]) for c in range(chunks))
 
     last = stages[-1]
-    feed = elementwise(fold_kernel, "fold", [feed[0], partner(feed[1], "seq", 1)], after=(last["attention"],))
+    feed = elementwise(fold_kernel, "fold", feed, after=(last["attention"],))
     finish(chunks - 1, after=(feed,))
     feed = to_chips(feed, "seq")
 
@@ -830,7 +812,7 @@
     )
     merged = elementwise(
         merge_kernel, "merge", [feed, heads[0], partner(heads[1], "seq", 1)],
-        (feed.shape[0], feed.shape[1] + heads[0].shape[1], LANES), times=100,
+        (feed.shape[0], feed.shape[1] + heads[0].shape[1], LANES),
     )
     merged = to_chips(merged, "seq")
     outer_grad, inner_wgrad = unpack(

time: 408 us -> 406 us (level)
  starting transfers between devices: 35.4 us -> 39.5 us
    ppermute x6 -> x7, waiting for transfers between devices: 17.6 us -> 17.5 us  [partner(): return lax.ppermute(array, axis, [(i, i ^ bit) for i in range(size)])]
  transfers between devices with their start and end apart: 20 -> 21, of which waited for: 11 -> 10; matrix products, arithmetic and copies ran while one was open for 8% -> 8% of each run, Pallas kernels for 38% -> 37%
where the time goes in v2:
time: 406 us; the launch traced here: 400 us
  Pallas kernels  153 us (38%)
  waiting for transfers between devices  96.6 us (24%)
  blocking collectives  54 us (13%)
  starting transfers between devices  39.5 us (10%)
  local copies, waits for them, and re-layouts  27.6 us (7%)
  between operations  15 us (4%)
  other arithmetic  14.5 us (4%)
    all_to_all x1, blocking collectives, to_chips(): lax.all_to_all(pieces, axis, 0, 0, tiled=True, axis_index_groups=groups)  41.3 us
    all_gather x2, waiting for transfers between devices, body(): token_parts = [lax.all_gather(own_tokens[c], 'tp') for c in range(chunks)]  32 us
    pallas_call x3, Pallas kernels, grads(): pl.pallas_call(behind(kernel, len(specs), after, 1), grid_spec=pltpu.Pref...  30.6 us
    all_to_all x6, starting transfers between devices, exchange(): lax.all_to_all(split, 'seq', 0, 0, tiled=True)  29.7 us
    all_to_all x6, waiting for transfers between devices, exchange(): lax.all_to_all(split, 'seq', 0, 0, tiled=True)  28.8 us
    pallas_call x2, Pallas kernels, dense_back(): pl.pallas_call(behind(dense_back_kernel, 10, after), grid=(total // rows,...  27.9 us
    pallas_call x2, Pallas kernels, attend(): pl.pallas_call(behind(partial(attend_kernel, tuple(sizes)), 7, after, 1),...  26 us
    pallas_call x2, Pallas kernels, norm_project(): pl.pallas_call(behind(norm_project_kernel, 10, after), grid=(total // row...  23.3 us
  transfers between devices with their start and end apart: 21, of which 10 were waited for; matrix products, arithmetic and copies ran while one was open for 8% of the time, Pallas kernels for 37%

profile of v2, /device:TPU:0, one launch (start us, length us, event | category | flops | bytes accessed | tf_op | source)
XLA Modules:
  0.0 399.8 jit_solution(13932758790858386875)
XLA Ops:
  12.7 12.7 %all_gather.16 = bf16[2,1024]{1,0:T(2,128)(2,1)S(1)} all-gather(bf16[2,256]{1,0:T(2,128)(2,1)S(1)} %pad_maximum_fusion.1), channel_id=1, replica_groups=mesh['seq'=8,'tp'=4] {'tp'}, dimensions={1}, use_global_device_ids=true | all-gather | bytes 5120 | tf_op jit(solution)/shard_map/all_gather | solution.py:720
  31.8 27.1 %all-gather.5.cloned.1.call-done.refs_0_.refs_3_ = bf16[4,1024,256]{2,1,0:T(8,128)(2,1)} async-done(((bf16[1,1024,256]{2,1,0:T(8,128)(2,1)}), bf16[4,1024,256]{2,1,0:T(8,128)(2,1)}) %all-gather.5.cloned.1.call-update) | async-done | bytes 2097168 | tf_op jit(solution)/shard_map/all_gather | solution.py:718
  59.0 11.7 %norm_project.2 = (bf16[1024,1024]{1,0:T(8,128)(2,1)}, bf16[1024,768]{1,0:T(8,128)(2,1)}, bf16[1024,1024]{1,0:T(8,128)(2,1)}, f32[1024,1024]{1,0:T(8,128)}, f32[1024,128]{1,0:T(8,128)}) custom-call(bf16[4,1024,256]{2,1,0:T(8,128)(2,1)} %all-gather.5.cloned.1.call-done.refs_0_.refs_3_, f32[1,1024]{1,0:T(1,128)} %get-tuple-element.113.refs_1_.refs_5_, ...), custom_call_target="tpu_custom_call" | custom-call | flops 11274289152 | bytes 36175872 | tf_op jit(solution)/shard_map/norm_project/pallas_call | solution.py:119
  95.9 9.4 %all-gather.7.cloned.1.call-done.refs_0_.refs_4_.refs_3_ = bf16[4,1024,256]{2,1,0:T(8,128)(2,1)} async-done(((bf16[1,1024,256]{2,1,0:T(8,128)(2,1)}), bf16[4,1024,256]{2,1,0:T(8,128)(2,1)}) %all-gather.7.cloned.1.call-update) | async-done | bytes 2097168 | tf_op jit(solution)/shard_map/all_gather | solution.py:719
  105.2 7.1 %push_back.2 = (bf16[1024,256]{1,0:T(8,128)(2,1)}, bf16[1024,1024]{1,0:T(8,128)(2,1)}, f32[1,1024]{1,0:T(1,128)}) custom-call(bf16[4,1024,256]{2,1,0:T(8,128)(2,1)} %all-gather.7.cloned.1.call-done.refs_0_.refs_4_.refs_3_, bf16[1024,256]{1,0:T(8,128)(2,1)} %bitcast.88, bf16[1024,1024]{1,0:T(8,128)(2,1)} %bitcast.77, f32[1024,1024]{1,0:T(8,128)} %get-tuple-element.51.refs_3_, ...), custom_call_target="tpu_custom_call" | custom-call | flops 8053063680 | bytes 26738688 | tf_op jit(solution)/shard_map/push_back/pallas_call | solution.py:182
  115.9 10.0 %feed_grads.2 = (bf16[4,2048,128]{2,1,0:T(8,128)(2,1)}, bf16[4,2048,128]{2,1,0:T(8,128)(2,1)}) custom-call(s32[1]{0:T(128)} %bitcast.20.refs_0_, bf16[1024,1024]{1,0:T(8,128)(2,1)} %get-tuple-element.53.refs_1_.refs_2_, bf16[1024,1024]{1,0:T(8,128)(2,1)} %get-tuple-element.54.refs_2_, bf16[1024,1024]{1,0:T(8,128)(2,1)} %get-tuple-element.55.refs_3_.refs_1_, ...), custom_call_target="tpu_custom_call" | custom-call | flops 12884901888 | bytes 25165824 | tf_op jit(solution)/shard_map/feed_grads/pallas_call | solution.py:499
  126.8 13.0 %attend.2.refs_10_ = bf16[1024,1024]{1,0:T(8,128)(2,1)} custom-call(s32[4]{0:T(128)} %get-tuple-element.91.refs_0_, bf16[1024,768]{1,0:T(8,128)(2,1)} %bitcast.7.refs_4_.refs_1_.refs_2_.refs_3_, bf16[1024,768]{1,0:T(8,128)(2,1)} %bitcast.7.refs_4_.refs_1_.refs_2_.refs_3_, bf16[1024,768]{1,0:T(8,128)(2,1)} %bitcast.7.refs_4_.refs_1_.refs_2_.refs_3_, ...), custom_call_target="tpu_custom_call" | custom-call | flops 9663676416 | bytes 12582912 | tf_op jit(solution)/shard_map/attend/pallas_call | solution.py:292
  152.1 11.7 %norm_project.3 = (bf16[1024,1024]{1,0:T(8,128)(2,1)}, bf16[1024,768]{1,0:T(8,128)(2,1)}, bf16[1024,1024]{1,0:T(8,128)(2,1)}, f32[1024,1024]{1,0:T(8,128)}, f32[1024,128]{1,0:T(8,128)}) custom-call(bf16[4,1024,256]{2,1,0:T(8,128)(2,1)} %all-gather.9.cloned.1.call-done.refs_0_.refs_3_, f32[1,1024]{1,0:T(1,128)} %get-tuple-element.113.refs_1_.refs_5_, ...), custom_call_target="tpu_custom_call" | custom-call | flops 11274289152 | bytes 36175872 | tf_op jit(solution)/shard_map/norm_project/pallas_call | solution.py:119
  163.7 8.0 %all-to-all-done.2 = bf16[8,128,1024]{2,1,0:T(8,128)(2,1)S(1)} async-done(((bf16[8,128,1024]{2,1,0:T(8,128)(2,1)}), bf16[8,128,1024]{2,1,0:T(8,128)(2,1)S(1)}, u32[]{:S(2)}, u32[]{:S(2)}) %all-to-all-start.2) | async-done | bytes 2097184 | tf_op jit(solution)/shard_map/all_to_all | solution.py:734
  176.1 14.0 %dense_back.2 = (bf16[4,2064,256]{2,1,0:T(8,128)(2,1)}, f32[2,1024]{1,0:T(2,128)}) custom-call(bf16[1024,1024]{1,0:T(8,128)(2,1)} %bitcast.61, bf16[1024,1024]{1,0:T(8,128)(2,1)} %get-tuple-element.55.refs_3_.refs_1_, bf16[1024,1024]{1,0:T(8,128)(2,1)} %get-tuple-element.53.refs_1_.refs_2_, ...), custom_call_target="tpu_custom_call" | custom-call | flops 19327352832 | bytes 37748736 | tf_op jit(solution)/shard_map/dense_back/pallas_call | solution.py:384
  190.1 7.9 %all-gather.11.cloned.1.call-done.refs_0_.refs_4_.refs_6_ = bf16[4,1024,256]{2,1,0:T(8,128)(2,1)} async-done(((bf16[1,1024,256]{2,1,0:T(8,128)(2,1)}), bf16[4,1024,256]{2,1,0:T(8,128)(2,1)}) %all-gather.11.cloned.1.call-update) | async-done | bytes 2097168 | tf_op jit(solution)/shard_map/all_gather | solution.py:719
  198.0 7.0 %push_back.3 = (bf16[1024,256]{1,0:T(8,128)(2,1)}, bf16[1024,1024]{1,0:T(8,128)(2,1)}, f32[1,1024]{1,0:T(1,128)}) custom-call(bf16[4,1024,256]{2,1,0:T(8,128)(2,1)} %all-gather.11.cloned.1.call-done.refs_0_.refs_4_.refs_6_, bf16[1024,256]{1,0:T(8,128)(2,1)} %bitcast.89, bf16[1024,1024]{1,0:T(8,128)(2,1)} %bitcast.78, ...), custom_call_target="tpu_custom_call" | custom-call | flops 53687091200 | bytes 178257920 | tf_op jit(solution)/shard_map/push_back/pallas_call | solution.py:182
  208.8 9.9 %feed_grads.3 = (bf16[4,2048,128]{2,1,0:T(8,128)(2,1)}, bf16[4,2048,128]{2,1,0:T(8,128)(2,1)}) custom-call(s32[1]{0:T(128)} %bitcast.20.refs_0_, bf16[1024,1024]{1,0:T(8,128)(2,1)} %get-tuple-element.63.refs_1_.refs_2_, bf16[1024,1024]{1,0:T(8,128)(2,1)} %get-tuple-element.58.refs_10_.refs_2_.refs_5_, bf16[1024,1024]{1,0:T(8,128)(2,1)} %get-tuple-element.64.refs_3_.refs_1_, ...), custom_call_target="tpu_custom_call" | custom-call | flops 12884901888 | bytes 25165824 | tf_op jit(solution)/shard_map/feed_grads/pallas_call | solution.py:499
  220.0 12.9 %attend.3.refs_4_ = bf16[1024,1024]{1,0:T(8,128)(2,1)} custom-call(s32[4]{0:T(128)} %get-tuple-element.90.refs_0_, bf16[1024,768]{1,0:T(8,128)(2,1)} %bitcast.28.refs_5_.refs_1_.refs_2_.refs_3_, bf16[1024,768]{1,0:T(8,128)(2,1)} %bitcast.28.refs_5_.refs_1_.refs_2_.refs_3_, bf16[1024,768]{1,0:T(8,128)(2,1)} %bitcast.28.refs_5_.refs_1_.refs_2_.refs_3_, ...), custom_call_target="tpu_custom_call" | custom-call | flops 9663676416 | bytes 12582912 | tf_op jit(solution)/shard_map/attend/pallas_call | solution.py:292
  232.9 8.3 %all-to-all-start.5 = ((bf16[8,128,1024]{2,1,0:T(8,128)(2,1)}), bf16[8,128,1024]{2,1,0:T(8,128)(2,1)S(1)}, u32[]{:S(2)}, u32[]{:S(2)}) async-start(bf16[8,128,1024]{2,1,0:T(8,128)(2,1)} %bitcast.65), calls=%async_computation.6 | async-start | bytes 4194304 | tf_op jit(solution)/shard_map/all_to_all | solution.py:734
  241.3 5.8 %fold.1.refs_10_ = bf16[4,2048,128]{2,1,0:T(8,128)(2,1)} custom-call(bf16[4,2048,128]{2,1,0:T(8,128)(2,1)} %get-tuple-element.56.refs_8_.refs_0_, bf16[4,2048,128]{2,1,0:T(8,128)(2,1)} %collective-permute-done.refs_1_, bf16[4,2048,128]{2,1,0:T(8,128)(2,1)} %get-tuple-element.65.refs_8_.refs_2_, bf16[4,2048,128]{2,1,0:T(8,128)(2,1)} %collective-permute-done.1.refs_3_, ...), custom_call_target="tpu_custom_call" | custom-call | flops 9437184 | bytes 18874368 | tf_op jit(solution)/shard_map/fold/pallas_call | solution.py:525
  247.1 20.8 %all-to-all-done.5 = bf16[8,128,1024]{2,1,0:T(8,128)(2,1)S(1)} async-done(((bf16[8,128,1024]{2,1,0:T(8,128)(2,1)}), bf16[8,128,1024]{2,1,0:T(8,128)(2,1)S(1)}, u32[]{:S(2)}, u32[]{:S(2)}) %all-to-all-start.5) | async-done | bytes 2097184 | tf_op jit(solution)/shard_map/all_to_all | solution.py:734
  269.2 14.0 %dense_back.3 = (bf16[4,2064,256]{2,1,0:T(8,128)(2,1)}, f32[2,1024]{1,0:T(2,128)}) custom-call(bf16[1024,1024]{1,0:T(8,128)(2,1)} %bitcast.63, bf16[1024,1024]{1,0:T(8,128)(2,1)} %get-tuple-element.64.refs_3_.refs_1_, bf16[1024,1024]{1,0:T(8,128)(2,1)} %get-tuple-element.63.refs_1_.refs_2_, ...), custom_call_target="tpu_custom_call" | custom-call | flops 19327352832 | bytes 37748736 | tf_op jit(solution)/shard_map/dense_back/pallas_call | solution.py:384
  287.2 6.2 %collective-permute-done.2 = f32[16,128]{1,0:T(8,128)S(1)} collective-permute-done((f32[16,128]{1,0:T(8,128)S(1)}, f32[16,128]{1,0:T(8,128)S(1)}, u32[]{:S(2)}, u32[]{:S(2)}) %collective-permute-start.2) | collective-permute-done | bytes 8224 | tf_op jit(solution)/shard_map/ppermute | solution.py:682
  293.8 5.5 %collective-permute-done.3 = f32[16,128]{1,0:T(8,128)S(1)} collective-permute-done((f32[16,128]{1,0:T(8,128)S(1)}, f32[16,128]{1,0:T(8,128)S(1)}, u32[]{:S(2)}, u32[]{:S(2)}) %collective-permute-start.3) | collective-permute-done | bytes 8224 | tf_op jit(solution)/shard_map/ppermute | solution.py:682
  300.0 10.7 %head_grads.1 = (bf16[4,1040,128]{2,1,0:T(8,128)(2,1)}, bf16[4,1040,128]{2,1,0:T(8,128)(2,1)}) custom-call(s32[1]{0:T(128)} %bitcast.20.refs_0_, bf16[1024,1024]{1,0:T(8,128)(2,1)} %bitcast.62, bf16[1024,1024]{1,0:T(8,128)(2,1)} %get-tuple-element.54.refs_2_, bf16[4,1024,256]{2,1,0:T(8,128)(2,1)} %all-gather.7.cloned.1.call-done.refs_0_.refs_4_.refs_3_, ...), custom_call_target="tpu_custom_call" | custom-call | tf_op jit(solution)/shard_map/head_grads/pallas_call | solution.py:499
  319.6 41.3 %all_to_all.45.refs_0_.refs_1_ = bf16[4,3088,128]{2,1,0:T(8,128)(2,1)S(1)} all-to-all(bf16[4,3088,128]{2,1,0:T(8,128)(2,1)} %merge.1), channel_id=1, replica_groups={{0,8,16,24},{4,12,20,28},{1,9,17,25},{5,13,21,29},{2,10,18,26},{6,14,22..., dimensions={0} | all-to-all | bytes 6324224 | tf_op jit(solution)/shard_map/all_to_all | solution.py:688
  371.1 7.0 %unpack.2 = (f32[1024,1024]{1,0:T(8,128)}, f32[1024,1024]{1,0:T(8,128)}) custom-call(s32[1]{0:T(128)} %bitcast.20.refs_0_, bf16[4,3088,128]{2,1,0:T(8,128)(2,1)} %copy-done, bf16[4,3088,128]{2,1,0:T(8,128)(2,1)} %collective-permute-done.5.refs_2_, bf16[2064,256]{1,0:T(8,128)(2,1)} %bitcast.70), custom_call_target="tpu_custom_call" | custom-call | flops 4743168 | bytes 56918016 | tf_op jit(solution)/shard_map/unpack/pallas_call | solution.py:598
  378.2 6.7 %last_step.1 = (bf16[128,16,256]{2,1,0:T(8,128)(2,1)}, f32[128,16,256]{2,1,0:T(8,128)}) custom-call(bf16[2064,256]{1,0:T(8,128)(2,1)} %bitcast.71, bf16[2064,256]{1,0:T(8,128)(2,1)} %bitcast.85, f32[8,128,128]{2,1,0:T(8,128)} %bitcast.86, f32[8,128,128]{2,1,0:T(8,128)} %bitcast.87, bf16[8,128,256]{2,1,0:T(8,128)(2,1)} %get-tuple-element.101.refs_4_, ...), custom_call_target="tpu_custom_call" | custom-call | flops 15728640 | bytes 9437184 | tf_op jit(solution)/shard_map/last_step/pallas_call | solution.py:656
  (142 shorter events, 96.1 us)
Async XLA Ops:
  7.2 51.8 %all-gather.5.cloned.1.call-start = ((), (), s32[]{:S(2)}) async-start(), calls=%async_computation.11 | async-start | bytes 2621440 | tf_op jit(solution)/shard_map/all_gather | solution.py:718
  10.0 95.2 %all-gather.7.cloned.1.call-start = ((), (), s32[]{:S(2)}) async-start(), calls=%async_computation.12 | async-start | bytes 2621440 | tf_op jit(solution)/shard_map/all_gather | solution.py:719
  70.6 34.6 %all-to-all-start = ((bf16[8,128,768]{2,1,0:T(8,128)(2,1)}), bf16[8,128,768]{2,1,0:T(8,128)(2,1)}, u32[]{:S(2)}, u32[]{:S(2)}) async-start(bf16[8,128,768]{2,1,0:T(8,128)(2,1)} %bitcast.83), calls=%async_computation | async-start | bytes 3145728 | tf_op jit(solution)/shard_map/all_to_all | solution.py:734
  75.1 77.0 %all-gather.9.cloned.1.call-start = ((), (), s32[]{:S(2)}) async-start(), calls=%async_computation.13 | async-start | bytes 2621440 | tf_op jit(solution)/shard_map/all_gather | solution.py:718
  112.3 13.7 %all-to-all-start.1 = ((bf16[8,128,256]{2,1,0:T(8,128)(2,1)}), bf16[8,128,256]{2,1,0:T(8,128)(2,1)S(1)}, u32[]{:S(2)}, u32[]{:S(2)}) async-start(bf16[8,128,256]{2,1,0:T(8,128)(2,1)} %bitcast.93), calls=%async_computation.1 | async-start | bytes 1048576 | tf_op jit(solution)/shard_map/all_to_all | solution.py:734
  139.8 31.9 %all-to-all-start.2 = ((bf16[8,128,1024]{2,1,0:T(8,128)(2,1)}), bf16[8,128,1024]{2,1,0:T(8,128)(2,1)S(1)}, u32[]{:S(2)}, u32[]{:S(2)}) async-start(bf16[8,128,1024]{2,1,0:T(8,128)(2,1)} %bitcast.79), calls=%async_computation.2 | async-start | bytes 4194304 | tf_op jit(solution)/shard_map/all_to_all | solution.py:734
  145.1 52.9 %all-gather.11.cloned.1.call-start = ((), (), s32[]{:S(2)}) async-start(), calls=%async_computation.15 | async-start | bytes 2621440 | tf_op jit(solution)/shard_map/all_gather | solution.py:719
  146.7 94.6 %collective-permute-start = (bf16[4,2048,128]{2,1,0:T(8,128)(2,1)}, bf16[4,2048,128]{2,1,0:T(8,128)(2,1)}, u32[]{:S(2)}, u32[]{:S(2)}) collective-permute-start(bf16[4,2048,128]{2,1,0:T(8,128)(2,1)} %get-tuple-element.67), channel_id=1, source_target_pairs={{0,4},{4,0},{8,12},{12,8},{16,20},{20,16},{24,28},{28,24},{1,5},{5... | collective-permute-start | bytes 6291464 | tf_op jit(solution)/shard_map/ppermute | solution.py:682
  171.7 26.3 %all-to-all-start.3 = ((bf16[8,128,768]{2,1,0:T(8,128)(2,1)}), bf16[8,128,768]{2,1,0:T(8,128)(2,1)}, u32[]{:S(2)}, u32[]{:S(2)}) async-start(bf16[8,128,768]{2,1,0:T(8,128)(2,1)} %bitcast.84), calls=%async_computation.4 | async-start | bytes 3145728 | tf_op jit(solution)/shard_map/all_to_all | solution.py:734
  176.0 195.1 %reduce-scatter.3.cloned.1.call-start = ((), (), s32[]{:S(2)}) async-start(), calls=%async_computation.14 | async-start | bytes 5283840 | tf_op jit(solution)/shard_map/reduce_scatter | solution.py:774
  205.0 14.2 %all-to-all-start.4 = ((bf16[8,128,256]{2,1,0:T(8,128)(2,1)}), bf16[8,128,256]{2,1,0:T(8,128)(2,1)S(1)}, u32[]{:S(2)}, u32[]{:S(2)}) async-start(bf16[8,128,256]{2,1,0:T(8,128)(2,1)} %bitcast.92), calls=%async_computation.5 | async-start | bytes 1048576 | tf_op jit(solution)/shard_map/all_to_all | solution.py:734
  218.7 22.6 %collective-permute-start.1 = (bf16[4,2048,128]{2,1,0:T(8,128)(2,1)}, bf16[4,2048,128]{2,1,0:T(8,128)(2,1)}, u32[]{:S(2)}, u32[]{:S(2)}) collective-permute-start(bf16[4,2048,128]{2,1,0:T(8,128)(2,1)} %get-tuple-element.68), channel_id=1, source_target_pairs={{0,4},{4,0},{8,12},{12,8},{16,20},{20,16},{24,28},{28,24},{1,5},{5... | collective-permute-start | bytes 6291464 | tf_op jit(solution)/shard_map/ppermute | solution.py:682
  232.9 34.9 %all-to-all-start.5 = ((bf16[8,128,1024]{2,1,0:T(8,128)(2,1)}), bf16[8,128,1024]{2,1,0:T(8,128)(2,1)S(1)}, u32[]{:S(2)}, u32[]{:S(2)}) async-start(bf16[8,128,1024]{2,1,0:T(8,128)(2,1)} %bitcast.65), calls=%async_computation.6 | async-start | bytes 4194304 | tf_op jit(solution)/shard_map/all_to_all | solution.py:734
  241.2 136.9 %reduce-scatter.5.cloned.1.call-start = ((), (), s32[]{:S(2)}) async-start(), calls=%async_computation.16 | async-start | bytes 5283840 | tf_op jit(solution)/shard_map/reduce_scatter | solution.py:774
  283.2 10.2 %copy-start.5 = (bf16[128,16,256]{2,1,0:T(8,128)(2,1)S(1)}, bf16[128,16,256]{2,1,0:T(8,128)(2,1)}, u32[]{:S(2)}) copy-start(bf16[128,16,256]{2,1,0:T(8,128)(2,1)} %param.27) | copy-start | bytes 3145732
  283.2 10.5 %copy-start.16 = (f32[1,1024]{1,0:T(1,128)S(1)}, f32[1,1024]{1,0:T(1,128)}, u32[]{:S(2)}) copy-start(f32[1,1024]{1,0:T(1,128)} %get-tuple-element.74) | copy-start | bytes 12292
  283.2 10.5 %copy-start.17 = (f32[1,1024]{1,0:T(1,128)S(1)}, f32[1,1024]{1,0:T(1,128)}, u32[]{:S(2)}) copy-start(f32[1,1024]{1,0:T(1,128)} %get-tuple-element.75) | copy-start | bytes 12292
  283.3 30.3 %all-to-all-start.6 = ((bf16[4,2048,128]{2,1,0:T(8,128)(2,1)}), bf16[4,2048,128]{2,1,0:T(8,128)(2,1)S(1)}, u32[]{:S(2)}, u32[]{:S(2)}) async-start(bf16[4,2048,128]{2,1,0:T(8,128)(2,1)} %fold.1.refs_10_), calls=%async_computation.8 | async-start | bytes 4194304 | tf_op jit(solution)/shard_map/all_to_all | solution.py:688
  287.1 6.3 %collective-permute-start.2 = (f32[16,128]{1,0:T(8,128)S(1)}, f32[16,128]{1,0:T(8,128)S(1)}, u32[]{:S(2)}, u32[]{:S(2)}) collective-permute-start(f32[16,128]{1,0:T(8,128)S(1)} %reshape.228), channel_id=1, source_target_pairs={{0,1},{1,0},{2,3},{3,2},{4,5},{5,4},{6,7},{7,6},{8,9},{9,8},{10,11... | collective-permute-start | bytes 24584 | tf_op jit(solution)/shard_map/ppermute | solution.py:682
  293.5 5.8 %collective-permute-start.3 = (f32[16,128]{1,0:T(8,128)S(1)}, f32[16,128]{1,0:T(8,128)S(1)}, u32[]{:S(2)}, u32[]{:S(2)}) collective-permute-start(f32[16,128]{1,0:T(8,128)S(1)} %add.128), channel_id=1, source_target_pairs={{0,2},{1,3},{2,0},{3,1},{4,6},{5,7},{6,4},{7,5},{8,10},{9,11},{10,... | collective-permute-start | bytes 24584 | tf_op jit(solution)/shard_map/ppermute | solution.py:682
  310.6 2.9 collective-permute-start.4
  360.9 10.2 %collective-permute-start.5 = (bf16[4,3088,128]{2,1,0:T(8,128)(2,1)S(1)}, bf16[4,3088,128]{2,1,0:T(8,128)(2,1)}, u32[]{:S(2)}, u32[]{:S(2)}) collective-permute-start(bf16[4,3088,128]{2,1,0:T(8,128)(2,1)S(1)} %all_to_all.45.refs_0_.refs_1_), channel_id=1, source_target_pairs={{0,4},{4,0},{8,12},{12,8},{16,20},{20,16},{24,28},{28,24},{1,5},{5... | collective-permute-start | bytes 9486344 | tf_op jit(solution)/shard_map/ppermute | solution.py:682
  365.6 19.3 %all-to-all-start.8 = ((bf16[4,1040,128]{2,1,0:T(8,128)(2,1)}), bf16[4,1040,128]{2,1,0:T(8,128)(2,1)}, u32[]{:S(2)}, u32[]{:S(2)}) async-start(bf16[4,1040,128]{2,1,0:T(8,128)(2,1)} %add_up.1), calls=%async_computation.10 | async-start | bytes 2129920 | tf_op jit(solution)/shard_map/all_to_all | solution.py:688
  384.9 3.0 collective-permute-start.6
  (22 other events, 67.5 us)
Sparse Core Ops, SparseCore 0:
  10.2 48.7 all-gather.4
  60.5 44.6 all-gather.6
  107.4 44.6 all-gather.8
  153.5 44.4 all-gather.10
  200.1 76.2 reduce-scatter.2
  283.3 74.5 reduce-scatter.4

commit v3 on v2

--- a/solution.py
+++ b/solution.py
@@ -72,8 +72,8 @@
 
 
 def norm_project_kernel(
-    x_ref, gain_ref, shift_ref, wq_ref, wk_ref, wv_ref, win_ref, bias_ref, cos_ref, sin_ref,
-    hidden_ref, qkv_ref, act_ref, slope_ref, stat_ref,
+    x_ref, gain_ref, shift_ref, wq_ref, wk_ref, wv_ref, win_ref, bias_ref, wout_ref, cos_ref, sin_ref,
+    hidden_ref, qkv_ref, act_ref, slope_ref, stat_ref, branch_ref,
 ):
     parts, rows, part = x_ref.shape
     width = parts * part
@@ -107,9 +107,10 @@
     slope_ref[...] = 0.5 * (1.0 + t) + 0.5 * v * (1.0 - t * t) * (
         GELU_A * (1.0 + 3.0 * GELU_B * square)
     )
-
-
-def norm_project(x, gain, shift, wq, wk, wv, win, bias, cos, sin, after=()):
+    branch_ref[...] = jnp.dot(act_ref[...], wout_ref[...], preferred_element_type=F32).astype(BF16)
+
+
+def norm_project(x, gain, shift, wq, wk, wv, win, bias, wout, cos, sin, after=()):
     parts, total, part = x.shape
     width, embed = wq.shape
     inner = win.shape[1]
@@ -117,7 +118,7 @@
     whole = lambda i: (0, 0)
     block = lambda i: (i, 0)
     return pl.pallas_call(
-        behind(norm_project_kernel, 10, after),
+        behind(norm_project_kernel, 11, after),
         grid=(total // rows,),
         in_specs=[
             pl.BlockSpec((parts, rows, part), lambda i: (0, i, 0)),
@@ -128,6 +129,7 @@
             pl.BlockSpec((width, embed), whole),
             pl.BlockSpec((width, inner), whole),
             pl.BlockSpec((1, inner), whole),
+            pl.BlockSpec((inner, width), whole),
             pl.BlockSpec((rows, LANES), block),
             pl.BlockSpec((rows, LANES), block),
             *unused(after),
@@ -138,6 +140,7 @@
             pl.BlockSpec((rows, inner), block),
             pl.BlockSpec((rows, inner), block),
             pl.BlockSpec((rows, LANES), block),
+            pl.BlockSpec((rows, width), block),
         ],
         out_shape=[
             jax.ShapeDtypeStruct((total, width), BF16),
@@ -145,11 +148,12 @@
             jax.ShapeDtypeStruct((total, inner), BF16),
             jax.ShapeDtypeStruct((total, inner), F32),
             jax.ShapeDtypeStruct((total, LANES), F32),
+            jax.ShapeDtypeStruct((total, width), BF16),
         ],
         compiler_params=params(),
         cost_estimate=work(2 * total * width * (3 * embed + inner), total * (4 * width + 6 * embed + 6 * inner)),
         name="norm_project",
-    )(x, gain, shift, wq, wk, wv, win, bias, cos, sin, *after)
+    )(x, gain, shift, wq, wk, wv, win, bias, wout, cos, sin, *after)
 
 
 def push_back_kernel(c_ref, wo_ref, wout_ref, slope_ref, mixed_grad_ref, inner_grad_ref, bias_ref):
@@ -315,7 +319,7 @@
 
 
 def dense_back_kernel(
-    back_ref, inner_ref, act_ref, x_ref, stat_ref, gain_ref, wqkv_ref, win_ref, wo_ref, wout_ref,
+    back_ref, inner_ref, branch_ref, x_ref, stat_ref, gain_ref, wqkv_ref, win_ref, wo_ref,
     out_ref, feature_ref, sums_ref,
 ):
     parts, rows, part = x_ref.shape
@@ -343,7 +347,7 @@
         out_ref[k, first, :] = total.astype(BF16)
         out_ref[k, second, :] = (
             jnp.dot(back_ref[:, pl.ds(0, embed)], wo_ref[:, at], preferred_element_type=F32)
-            + jnp.dot(act_ref[...], wout_ref[:, at], preferred_element_type=F32)
+            + branch_ref[:, at].astype(F32)
         ).astype(BF16)
         scaled = (x_ref[k].astype(F32) - mean) * inverse
         product = total * scaled
@@ -373,7 +377,7 @@
     return -(-2 * total // part // 16) * 16
 
 
-def dense_back(back, inner_grad, act, x, stat, gain, wqkv, win, wo, wout, after=()):
+def dense_back(back, inner_grad, branch, x, stat, gain, wqkv, win, wo, after=()):
     parts, total, part = x.shape
     embed, width = wo.shape
     inner = win.shape[0]
@@ -382,19 +386,18 @@
     whole = lambda i: (0, 0)
     block = lambda i: (i, 0)
     return pl.pallas_call(
-        behind(dense_back_kernel, 10, after),
+        behind(dense_back_kernel, 9, after),
         grid=(total // rows,),
         in_specs=[
             pl.BlockSpec((rows, 4 * embed), block),
             pl.BlockSpec((rows, inner), block),
-            pl.BlockSpec((rows, inner), block),
+            pl.BlockSpec((rows, width), block),
             pl.BlockSpec((parts, rows, part), lambda i: (0, i, 0)),
             pl.BlockSpec((rows, LANES), block),
             pl.BlockSpec((1, width), whole),
             pl.BlockSpec((3 * embed, width), whole),
             pl.BlockSpec((inner, width), whole),
             pl.BlockSpec((embed, width), whole),
-            pl.BlockSpec((inner, width), whole),
             *unused(after),
         ],
         out_specs=[
@@ -409,7 +412,7 @@
         compiler_params=params(),
         cost_estimate=work(2 * total * width * (4 * embed + 2 * inner), total * (6 * width + 8 * embed + 4 * inner)),
         name="dense_back",
-    )(back, inner_grad, act, x, stat, gain, wqkv, win, wo, wout, *after)
+    )(back, inner_grad, branch, x, stat, gain, wqkv, win, wo, *after)
 
 
 def tn_dot(left, right):
@@ -710,7 +713,7 @@
     chunks = batch_rows // seq_count
 
     own_tokens, own_cotangent = (
-        [part.reshape(extent, local_width) for part in jnp.split(jnp.swapaxes(array, 0, 1), chunks)]
+        [jnp.swapaxes(part, 0, 1).reshape(extent, local_width) for part in jnp.split(array, chunks, axis=1)]
         for array in (tokens, cotangent)
     )
     back_qkv = jnp.concatenate([w.T for w in (query_weight, key_weight, value_weight)], axis=0)
@@ -739,9 +742,9 @@
 
     def project(c, after=()):
         o = stages[c]
-        o["hidden"], qkv, o["act"], o["slope"], o["stat"] = norm_project(
+        o["hidden"], qkv, o["act"], o["slope"], o["stat"], o["branch"] = norm_project(
             token_parts[c], gain, shift, query_weight, key_weight, value_weight, inner_weight,
-            bias_row, own_cos[c], own_sin[c], after=after,
+            bias_row, outer_weight, own_cos[c], own_sin[c], after=after,
         )
         o["qkv_rows"] = exchange(qkv)
 
@@ -768,8 +771,8 @@
     def finish(c, after=()):
         o = stages[c]
         o["made"], o["feature"] = dense_back(
-            o["back"], o["inner_grad"], o["act"], token_parts[c], o["stat"], gain, back_qkv, back_inner,
-            output_weight, outer_weight, after=after,
+            o["back"], o["inner_grad"], o["branch"], token_parts[c], o["stat"], gain, back_qkv, back_inner,
+            output_weight, after=after,
         )
         o["both"] = lax.psum_scatter(o["made"], "tp", scatter_dimension=0)
 

time: 406 us -> 400 us (0.985)
  waiting for transfers between devices: 96.6 us -> 86.9 us
    all_gather x2, waiting for transfers between devices: 17.2 us -> 12.3 us  [body(): lax.all_gather(own_cotangent[c], 'tp')]
    ppermute x7, waiting for transfers between devices: 17.5 us -> 13 us  [partner(): return lax.ppermute(array, axis, [(i, i ^ bit) for i in range(size)])]
    unnamed x60 -> x58, local copies, waits for them, and re-layouts: 20.5 us -> 20.1 us
  transfers between devices with their start and end apart: 21 -> 21, of which waited for: 10 -> 12; matrix products, arithmetic and copies ran while one was open for 8% -> 9% of each run, Pallas kernels for 37% -> 38%
where the time goes in v3:
time: 400 us; the launch traced here: 392 us
  Pallas kernels  154 us (38%)
  waiting for transfers between devices  86.9 us (22%)
  blocking collectives  53.1 us (13%)
  starting transfers between devices  38.7 us (10%)
  local copies, waits for them, and re-layouts  30 us (8%)
  between operations  15 us (4%)
  other arithmetic  14.6 us (4%)
    all_to_all x1, blocking collectives, to_chips(): lax.all_to_all(pieces, axis, 0, 0, tiled=True, axis_index_groups=groups)  40.5 us
    pallas_call x3, Pallas kernels, grads(): pl.pallas_call(behind(kernel, len(specs), after, 1), grid_spec=pltpu.Pref...  30.6 us
    all_to_all x6, waiting for transfers between devices, exchange(): lax.all_to_all(split, 'seq', 0, 0, tiled=True)  30.4 us
    all_gather x2, waiting for transfers between devices, body(): token_parts = [lax.all_gather(own_tokens[c], 'tp') for c in range(chunks)]  29.7 us
    pallas_call x2, Pallas kernels, norm_project(): pl.pallas_call(behind(norm_project_kernel, 11, after), grid=(total // row...  29.1 us
    all_to_all x6, starting transfers between devices, exchange(): lax.all_to_all(split, 'seq', 0, 0, tiled=True)  28.2 us
    pallas_call x2, Pallas kernels, attend(): pl.pallas_call(behind(partial(attend_kernel, tuple(sizes)), 7, after, 1),...  27.1 us
    pallas_call x2, Pallas kernels, dense_back(): pl.pallas_call(behind(dense_back_kernel, 9, after), grid=(total // rows,)...  22.4 us
  transfers between devices with their start and end apart: 21, of which 12 were waited for; matrix products, arithmetic and copies ran while one was open for 9% of the time, Pallas kernels for 38%

profile of v3, /device:TPU:0, one launch (start us, length us, event | category | flops | bytes accessed | tf_op | source)
XLA Modules:
  0.0 392.1 jit_solution(18027907119200549624)
XLA Ops:
  11.8 12.6 %all_gather.16 = bf16[2,1024]{1,0:T(2,128)(2,1)S(1)} all-gather(bf16[2,256]{1,0:T(2,128)(2,1)S(1)} %pad_maximum_fusion.1), channel_id=1, replica_groups=mesh['seq'=8,'tp'=4] {'tp'}, dimensions={1}, use_global_device_ids=true | all-gather | bytes 5120 | tf_op jit(solution)/shard_map/all_gather | solution.py:723
  30.8 28.0 %all-gather.5.cloned.1.call-done.refs_0_.refs_3_ = bf16[4,1024,256]{2,1,0:T(8,128)(2,1)} async-done(((bf16[1,1024,256]{2,1,0:T(8,128)(2,1)}), bf16[4,1024,256]{2,1,0:T(8,128)(2,1)}) %all-gather.5.cloned.1.call-update) | async-done | bytes 2097168 | tf_op jit(solution)/shard_map/all_gather | solution.py:721
  58.8 14.4 %norm_project.2 = (bf16[1024,1024]{1,0:T(8,128)(2,1)}, bf16[1024,768]{1,0:T(8,128)(2,1)}, bf16[1024,1024]{1,0:T(8,128)(2,1)}, f32[1024,1024]{1,0:T(8,128)}, f32[...) custom-call(bf16[4,1024,256]{2,1,0:T(8,128)(2,1)} %all-gather.5.cloned.1.call-done.refs_0_.refs_3_, ...), custom_call_target="tpu_custom_call" | custom-call | flops 11274289152 | bytes 36175872 | tf_op jit(solution)/shard_map/norm_project/pallas_call | solution.py:120
  95.3 5.6 %fusion.2 = (f32[1024,128]{1,0:T(8,128)}, f32[1024,128]{1,0:T(8,128)}, f32[1024,128]{1,0:T(8,128)}, f32[1024,128]{1,0:T(8,128)}) fusion(f32[1024]{0:T(1024)S(1)} %bitcast.106, f32[128]{0:T(128)S(1)} %get-tuple-element.130, f32[128]{0:T(128)S(1)} %get-tuple-element.131, f32[1024]{0:T(1024)S(1)} %bitcast.107), kind=kLoop, calls=%fused_computation.10 | loop fusion | flops 524288 | bytes 2106368 | tf_op jit(solution)/shard_map/mul | solution.py:66
  105.1 7.0 %push_back.2 = (bf16[1024,256]{1,0:T(8,128)(2,1)}, bf16[1024,1024]{1,0:T(8,128)(2,1)}, f32[1,1024]{1,0:T(1,128)}) custom-call(bf16[4,1024,256]{2,1,0:T(8,128)(2,1)} %all-gather.7.cloned.1.call-done.refs_0_.refs_4_.refs_3_, bf16[1024,256]{1,0:T(8,128)(2,1)} %bitcast.100, bf16[1024,1024]{1,0:T(8,128)(2,1)} %bitcast.89, ...), custom_call_target="tpu_custom_call" | custom-call | flops 8053063680 | bytes 26738688 | tf_op jit(solution)/shard_map/push_back/pallas_call | solution.py:186
  115.8 9.9 %feed_grads.2 = (bf16[4,2048,128]{2,1,0:T(8,128)(2,1)}, bf16[4,2048,128]{2,1,0:T(8,128)(2,1)}) custom-call(s32[1]{0:T(128)} %bitcast.20.refs_0_, bf16[1024,1024]{1,0:T(8,128)(2,1)} %get-tuple-element.55.refs_1_, bf16[1024,1024]{1,0:T(8,128)(2,1)} %get-tuple-element.56.refs_2_, bf16[1024,1024]{1,0:T(8,128)(2,1)} %get-tuple-element.57.refs_3_.refs_1_, ...), custom_call_target="tpu_custom_call" | custom-call | flops 12884901888 | bytes 25165824 | tf_op jit(solution)/shard_map/feed_grads/pallas_call | solution.py:502
  126.5 13.1 %attend.2.refs_11_ = bf16[1024,1024]{1,0:T(8,128)(2,1)} custom-call(s32[4]{0:T(128)} %get-tuple-element.95.refs_0_, bf16[1024,768]{1,0:T(8,128)(2,1)} %bitcast.7.refs_4_.refs_1_.refs_2_.refs_3_, bf16[1024,768]{1,0:T(8,128)(2,1)} %bitcast.7.refs_4_.refs_1_.refs_2_.refs_3_, bf16[1024,768]{1,0:T(8,128)(2,1)} %bitcast.7.refs_4_.refs_1_.refs_2_.refs_3_, ...), custom_call_target="tpu_custom_call" | custom-call | flops 9663676416 | bytes 12582912 | tf_op jit(solution)/shard_map/attend/pallas_call | solution.py:296
  139.6 7.5 %all-to-all-start.2 = ((bf16[8,128,1024]{2,1,0:T(8,128)(2,1)}), bf16[8,128,1024]{2,1,0:T(8,128)(2,1)S(1)}, u32[]{:S(2)}, u32[]{:S(2)}) async-start(bf16[8,128,1024]{2,1,0:T(8,128)(2,1)} %bitcast.91), calls=%async_computation.2 | async-start | bytes 4194304 | tf_op jit(solution)/shard_map/all_to_all | solution.py:737
  151.3 14.6 %norm_project.3 = (bf16[1024,1024]{1,0:T(8,128)(2,1)}, bf16[1024,768]{1,0:T(8,128)(2,1)}, bf16[1024,1024]{1,0:T(8,128)(2,1)}, f32[1024,1024]{1,0:T(8,128)}, f32[...) custom-call(bf16[4,1024,256]{2,1,0:T(8,128)(2,1)} %all-gather.9.cloned.1.call-done.refs_0_.refs_3_, ...), custom_call_target="tpu_custom_call" | custom-call | flops 11274289152 | bytes 36175872 | tf_op jit(solution)/shard_map/norm_project/pallas_call | solution.py:120
  165.9 7.9 %all-to-all-done.2 = bf16[8,128,1024]{2,1,0:T(8,128)(2,1)S(1)} async-done(((bf16[8,128,1024]{2,1,0:T(8,128)(2,1)}), bf16[8,128,1024]{2,1,0:T(8,128)(2,1)S(1)}, u32[]{:S(2)}, u32[]{:S(2)}) %all-to-all-start.2) | async-done | bytes 2097184 | tf_op jit(solution)/shard_map/all_to_all | solution.py:737
  178.1 11.2 %dense_back.2 = (bf16[4,2064,256]{2,1,0:T(8,128)(2,1)}, f32[2,1024]{1,0:T(2,128)}) custom-call(bf16[1024,1024]{1,0:T(8,128)(2,1)} %bitcast.71, bf16[1024,1024]{1,0:T(8,128)(2,1)} %get-tuple-element.57.refs_3_.refs_1_, bf16[1024,1024]{1,0:T(8,128)(2,1)} %get-tuple-element.59.refs_2_, bf16[4,1024,256]{2,1,0:T(8,128)(2,1)} %all-gather.5.cloned.1.call-done.refs_0_.refs_3_, ...), custom_call_target="tpu_custom_call" | custom-call | flops 19327352832 | bytes 37748736 | tf_op jit(solution)/shard_map/dense_back/pallas_call | solution.py:388
  189.3 8.1 %all-gather.11.cloned.1.call-done.refs_0_.refs_4_.refs_6_ = bf16[4,1024,256]{2,1,0:T(8,128)(2,1)} async-done(((bf16[1,1024,256]{2,1,0:T(8,128)(2,1)}), bf16[4,1024,256]{2,1,0:T(8,128)(2,1)}) %all-gather.11.cloned.1.call-update) | async-done | bytes 2097168 | tf_op jit(solution)/shard_map/all_gather | solution.py:722
  199.1 7.0 %push_back.3 = (bf16[1024,256]{1,0:T(8,128)(2,1)}, bf16[1024,1024]{1,0:T(8,128)(2,1)}, f32[1,1024]{1,0:T(1,128)}) custom-call(bf16[4,1024,256]{2,1,0:T(8,128)(2,1)} %all-gather.11.cloned.1.call-done.refs_0_.refs_4_.refs_6_, bf16[1024,256]{1,0:T(8,128)(2,1)} %bitcast.101, bf16[1024,1024]{1,0:T(8,128)(2,1)} %bitcast.90, ...), custom_call_target="tpu_custom_call" | custom-call | flops 53687091200 | bytes 178257920 | tf_op jit(solution)/shard_map/push_back/pallas_call | solution.py:186
  209.6 10.0 %feed_grads.3 = (bf16[4,2048,128]{2,1,0:T(8,128)(2,1)}, bf16[4,2048,128]{2,1,0:T(8,128)(2,1)}) custom-call(s32[1]{0:T(128)} %bitcast.20.refs_0_, bf16[1024,1024]{1,0:T(8,128)(2,1)} %get-tuple-element.66.refs_1_, bf16[1024,1024]{1,0:T(8,128)(2,1)} %get-tuple-element.61.refs_9_.refs_2_.refs_5_, bf16[1024,1024]{1,0:T(8,128)(2,1)} %get-tuple-element.67.refs_3_.refs_1_, ...), custom_call_target="tpu_custom_call" | custom-call | flops 12884901888 | bytes 25165824 | tf_op jit(solution)/shard_map/feed_grads/pallas_call | solution.py:502
  220.8 14.0 %attend.3.refs_4_ = bf16[1024,1024]{1,0:T(8,128)(2,1)} custom-call(s32[4]{0:T(128)} %get-tuple-element.94.refs_0_, bf16[1024,768]{1,0:T(8,128)(2,1)} %bitcast.29.refs_5_.refs_1_.refs_2_.refs_3_, bf16[1024,768]{1,0:T(8,128)(2,1)} %bitcast.29.refs_5_.refs_1_.refs_2_.refs_3_, bf16[1024,768]{1,0:T(8,128)(2,1)} %bitcast.29.refs_5_.refs_1_.refs_2_.refs_3_, ...), custom_call_target="tpu_custom_call" | custom-call | flops 9663676416 | bytes 12582912 | tf_op jit(solution)/shard_map/attend/pallas_call | solution.py:296
  234.9 4.9 %all-to-all-start.5 = ((bf16[8,128,1024]{2,1,0:T(8,128)(2,1)}), bf16[8,128,1024]{2,1,0:T(8,128)(2,1)S(1)}, u32[]{:S(2)}, u32[]{:S(2)}) async-start(bf16[8,128,1024]{2,1,0:T(8,128)(2,1)} %bitcast.75), calls=%async_computation.6 | async-start | bytes 4194304 | tf_op jit(solution)/shard_map/all_to_all | solution.py:737
  239.9 5.8 %fold.1.refs_9_ = bf16[4,2048,128]{2,1,0:T(8,128)(2,1)} custom-call(bf16[4,2048,128]{2,1,0:T(8,128)(2,1)} %get-tuple-element.58.refs_8_.refs_0_, bf16[4,2048,128]{2,1,0:T(8,128)(2,1)} %collective-permute-done.refs_1_, bf16[4,2048,128]{2,1,0:T(8,128)(2,1)} %get-tuple-element.68.refs_8_.refs_2_, bf16[4,2048,128]{2,1,0:T(8,128)(2,1)} %collective-permute-done.1.refs_3_, ...), custom_call_target="tpu_custom_call" | custom-call | flops 9437184 | bytes 18874368 | tf_op jit(solution)/shard_map/fold/pallas_call | solution.py:528
  245.7 20.8 %all-to-all-done.5 = bf16[8,128,1024]{2,1,0:T(8,128)(2,1)S(1)} async-done(((bf16[8,128,1024]{2,1,0:T(8,128)(2,1)}), bf16[8,128,1024]{2,1,0:T(8,128)(2,1)S(1)}, u32[]{:S(2)}, u32[]{:S(2)}) %all-to-all-start.5) | async-done | bytes 2097184 | tf_op jit(solution)/shard_map/all_to_all | solution.py:737
  267.8 11.2 %dense_back.3 = (bf16[4,2064,256]{2,1,0:T(8,128)(2,1)}, f32[2,1024]{1,0:T(2,128)}) custom-call(bf16[1024,1024]{1,0:T(8,128)(2,1)} %bitcast.73, bf16[1024,1024]{1,0:T(8,128)(2,1)} %get-tuple-element.67.refs_3_.refs_1_, bf16[1024,1024]{1,0:T(8,128)(2,1)} %get-tuple-element.69.refs_2_, bf16[4,1024,256]{2,1,0:T(8,128)(2,1)} %all-gather.9.cloned.1.call-done.refs_0_.refs_3_, ...), custom_call_target="tpu_custom_call" | custom-call | flops 19327352832 | bytes 37748736 | tf_op jit(solution)/shard_map/dense_back/pallas_call | solution.py:388
  292.1 10.7 %head_grads.1 = (bf16[4,1040,128]{2,1,0:T(8,128)(2,1)}, bf16[4,1040,128]{2,1,0:T(8,128)(2,1)}) custom-call(s32[1]{0:T(128)} %bitcast.20.refs_0_, bf16[1024,1024]{1,0:T(8,128)(2,1)} %bitcast.72, bf16[1024,1024]{1,0:T(8,128)(2,1)} %get-tuple-element.56.refs_2_, bf16[4,1024,256]{2,1,0:T(8,128)(2,1)} %all-gather.7.cloned.1.call-done.refs_0_.refs_4_.refs_3_, ...), custom_call_target="tpu_custom_call" | custom-call | tf_op jit(solution)/shard_map/head_grads/pallas_call | solution.py:502
  312.7 40.5 %all_to_all.45.refs_0_.refs_1_ = bf16[4,3088,128]{2,1,0:T(8,128)(2,1)S(1)} all-to-all(bf16[4,3088,128]{2,1,0:T(8,128)(2,1)} %merge.1), channel_id=1, replica_groups={{0,8,16,24},{4,12,20,28},{1,9,17,25},{5,13,21,29},{2,10,18,26},{6,14,22..., dimensions={0} | all-to-all | bytes 6324224 | tf_op jit(solution)/shard_map/all_to_all | solution.py:691
  358.0 4.4 %all-to-all-start.8 = ((bf16[4,1040,128]{2,1,0:T(8,128)(2,1)}), bf16[4,1040,128]{2,1,0:T(8,128)(2,1)}, u32[]{:S(2)}, u32[]{:S(2)}) async-start(bf16[4,1040,128]{2,1,0:T(8,128)(2,1)} %add_up.1), calls=%async_computation.10 | async-start | bytes 2129920 | tf_op jit(solution)/shard_map/all_to_all | solution.py:691
  363.5 7.0 %unpack.2 = (f32[1024,1024]{1,0:T(8,128)}, f32[1024,1024]{1,0:T(8,128)}) custom-call(s32[1]{0:T(128)} %bitcast.20.refs_0_, bf16[4,3088,128]{2,1,0:T(8,128)(2,1)} %copy-done, bf16[4,3088,128]{2,1,0:T(8,128)(2,1)} %collective-permute-done.5.refs_2_, bf16[2064,256]{1,0:T(8,128)(2,1)} %bitcast.84), custom_call_target="tpu_custom_call" | custom-call | flops 4743168 | bytes 56918016 | tf_op jit(solution)/shard_map/unpack/pallas_call | solution.py:601
  370.6 6.7 %last_step.1 = (bf16[128,16,256]{2,1,0:T(8,128)(2,1)}, f32[128,16,256]{2,1,0:T(8,128)}) custom-call(bf16[2064,256]{1,0:T(8,128)(2,1)} %bitcast.85, bf16[2064,256]{1,0:T(8,128)(2,1)} %bitcast.97, f32[8,128,128]{2,1,0:T(8,128)} %bitcast.98, f32[8,128,128]{2,1,0:T(8,128)} %bitcast.99, bf16[8,128,256]{2,1,0:T(8,128)(2,1)} %bitcast.77, ...), custom_call_target="tpu_custom_call" | custom-call | flops 15728640 | bytes 9437184 | tf_op jit(solution)/shard_map/last_step/pallas_call | solution.py:659
  (144 shorter events, 94.1 us)
Async XLA Ops:
  7.2 51.6 %all-gather.5.cloned.1.call-start = ((), (), s32[]{:S(2)}) async-start(), calls=%async_computation.11 | async-start | bytes 2621440 | tf_op jit(solution)/shard_map/all_gather | solution.py:721
  9.5 95.5 %all-gather.7.cloned.1.call-start = ((), (), s32[]{:S(2)}) async-start(), calls=%async_computation.12 | async-start | bytes 2621440 | tf_op jit(solution)/shard_map/all_gather | solution.py:722
  73.3 31.8 %all-to-all-start = ((bf16[8,128,768]{2,1,0:T(8,128)(2,1)}), bf16[8,128,768]{2,1,0:T(8,128)(2,1)}, u32[]{:S(2)}, u32[]{:S(2)}) async-start(bf16[8,128,768]{2,1,0:T(8,128)(2,1)} %bitcast.95), calls=%async_computation | async-start | bytes 3145728 | tf_op jit(solution)/shard_map/all_to_all | solution.py:737
  77.6 73.7 %all-gather.9.cloned.1.call-start = ((), (), s32[]{:S(2)}) async-start(), calls=%async_computation.13 | async-start | bytes 2621440 | tf_op jit(solution)/shard_map/all_gather | solution.py:721
  112.1 13.6 %all-to-all-start.1 = ((bf16[8,128,256]{2,1,0:T(8,128)(2,1)}), bf16[8,128,256]{2,1,0:T(8,128)(2,1)S(1)}, u32[]{:S(2)}, u32[]{:S(2)}) async-start(bf16[8,128,256]{2,1,0:T(8,128)(2,1)} %bitcast.105), calls=%async_computation.1 | async-start | bytes 1048576 | tf_op jit(solution)/shard_map/all_to_all | solution.py:737
  139.6 34.2 %all-to-all-start.2 = ((bf16[8,128,1024]{2,1,0:T(8,128)(2,1)}), bf16[8,128,1024]{2,1,0:T(8,128)(2,1)S(1)}, u32[]{:S(2)}, u32[]{:S(2)}) async-start(bf16[8,128,1024]{2,1,0:T(8,128)(2,1)} %bitcast.91), calls=%async_computation.2 | async-start | bytes 4194304 | tf_op jit(solution)/shard_map/all_to_all | solution.py:737
  147.1 50.3 %all-gather.11.cloned.1.call-start = ((), (), s32[]{:S(2)}) async-start(), calls=%async_computation.15 | async-start | bytes 2621440 | tf_op jit(solution)/shard_map/all_gather | solution.py:722
  149.1 90.7 %collective-permute-start = (bf16[4,2048,128]{2,1,0:T(8,128)(2,1)}, bf16[4,2048,128]{2,1,0:T(8,128)(2,1)}, u32[]{:S(2)}, u32[]{:S(2)}) collective-permute-start(bf16[4,2048,128]{2,1,0:T(8,128)(2,1)} %get-tuple-element.71), channel_id=1, source_target_pairs={{0,4},{4,0},{8,12},{12,8},{16,20},{20,16},{24,28},{28,24},{1,5},{5... | collective-permute-start | bytes 6291464 | tf_op jit(solution)/shard_map/ppermute | solution.py:685
  173.8 25.3 %all-to-all-start.3 = ((bf16[8,128,768]{2,1,0:T(8,128)(2,1)}), bf16[8,128,768]{2,1,0:T(8,128)(2,1)}, u32[]{:S(2)}, u32[]{:S(2)}) async-start(bf16[8,128,768]{2,1,0:T(8,128)(2,1)} %bitcast.96), calls=%async_computation.4 | async-start | bytes 3145728 | tf_op jit(solution)/shard_map/all_to_all | solution.py:737
  178.1 185.5 %reduce-scatter.3.cloned.1.call-start = ((), (), s32[]{:S(2)}) async-start(), calls=%async_computation.14 | async-start | bytes 5283840 | tf_op jit(solution)/shard_map/reduce_scatter | solution.py:777
  206.1 13.9 %all-to-all-start.4 = ((bf16[8,128,256]{2,1,0:T(8,128)(2,1)}), bf16[8,128,256]{2,1,0:T(8,128)(2,1)S(1)}, u32[]{:S(2)}, u32[]{:S(2)}) async-start(bf16[8,128,256]{2,1,0:T(8,128)(2,1)} %bitcast.104), calls=%async_computation.5 | async-start | bytes 1048576 | tf_op jit(solution)/shard_map/all_to_all | solution.py:737
  219.7 20.2 %collective-permute-start.1 = (bf16[4,2048,128]{2,1,0:T(8,128)(2,1)}, bf16[4,2048,128]{2,1,0:T(8,128)(2,1)}, u32[]{:S(2)}, u32[]{:S(2)}) collective-permute-start(bf16[4,2048,128]{2,1,0:T(8,128)(2,1)} %get-tuple-element.72), channel_id=1, source_target_pairs={{0,4},{4,0},{8,12},{12,8},{16,20},{20,16},{24,28},{28,24},{1,5},{5... | collective-permute-start | bytes 6291464 | tf_op jit(solution)/shard_map/ppermute | solution.py:685
  234.9 31.6 %all-to-all-start.5 = ((bf16[8,128,1024]{2,1,0:T(8,128)(2,1)}), bf16[8,128,1024]{2,1,0:T(8,128)(2,1)S(1)}, u32[]{:S(2)}, u32[]{:S(2)}) async-start(bf16[8,128,1024]{2,1,0:T(8,128)(2,1)} %bitcast.75), calls=%async_computation.6 | async-start | bytes 4194304 | tf_op jit(solution)/shard_map/all_to_all | solution.py:737
  239.8 130.8 %reduce-scatter.5.cloned.1.call-start = ((), (), s32[]{:S(2)}) async-start(), calls=%async_computation.16 | async-start | bytes 5283840 | tf_op jit(solution)/shard_map/reduce_scatter | solution.py:777
  279.1 8.5 %copy-start.5 = (bf16[128,16,256]{2,1,0:T(8,128)(2,1)S(1)}, bf16[128,16,256]{2,1,0:T(8,128)(2,1)}, u32[]{:S(2)}) copy-start(bf16[128,16,256]{2,1,0:T(8,128)(2,1)} %param.27) | copy-start | bytes 3145732
  279.1 8.7 %copy-start.16 = (f32[1,1024]{1,0:T(1,128)S(1)}, f32[1,1024]{1,0:T(1,128)}, u32[]{:S(2)}) copy-start(f32[1,1024]{1,0:T(1,128)} %get-tuple-element.78) | copy-start | bytes 12292
  279.1 8.7 %copy-start.17 = (f32[1,1024]{1,0:T(1,128)S(1)}, f32[1,1024]{1,0:T(1,128)}, u32[]{:S(2)}) copy-start(f32[1,1024]{1,0:T(1,128)} %get-tuple-element.79) | copy-start | bytes 12292
  279.1 28.0 %all-to-all-start.6 = ((bf16[4,2048,128]{2,1,0:T(8,128)(2,1)}), bf16[4,2048,128]{2,1,0:T(8,128)(2,1)S(1)}, u32[]{:S(2)}, u32[]{:S(2)}) async-start(bf16[4,2048,128]{2,1,0:T(8,128)(2,1)} %fold.1.refs_9_), calls=%async_computation.8 | async-start | bytes 4194304 | tf_op jit(solution)/shard_map/all_to_all | solution.py:691
  282.9 3.7 collective-permute-start.2
  286.6 4.8 %collective-permute-start.3 = (f32[16,128]{1,0:T(8,128)S(1)}, f32[16,128]{1,0:T(8,128)S(1)}, u32[]{:S(2)}, u32[]{:S(2)}) collective-permute-start(f32[16,128]{1,0:T(8,128)S(1)} %add.128), channel_id=1, source_target_pairs={{0,2},{1,3},{2,0},{3,1},{4,6},{5,7},{6,4},{7,5},{8,10},{9,11},{10,... | collective-permute-start | bytes 24584 | tf_op jit(solution)/shard_map/ppermute | solution.py:685
  302.8 2.9 collective-permute-start.4
  353.2 10.3 %collective-permute-start.5 = (bf16[4,3088,128]{2,1,0:T(8,128)(2,1)S(1)}, bf16[4,3088,128]{2,1,0:T(8,128)(2,1)}, u32[]{:S(2)}, u32[]{:S(2)}) collective-permute-start(bf16[4,3088,128]{2,1,0:T(8,128)(2,1)S(1)} %all_to_all.45.refs_0_.refs_1_), channel_id=1, source_target_pairs={{0,4},{4,0},{8,12},{12,8},{16,20},{20,16},{24,28},{28,24},{1,5},{5... | collective-permute-start | bytes 9486344 | tf_op jit(solution)/shard_map/ppermute | solution.py:685
  358.0 19.3 %all-to-all-start.8 = ((bf16[4,1040,128]{2,1,0:T(8,128)(2,1)}), bf16[4,1040,128]{2,1,0:T(8,128)(2,1)}, u32[]{:S(2)}, u32[]{:S(2)}) async-start(bf16[4,1040,128]{2,1,0:T(8,128)(2,1)} %add_up.1), calls=%async_computation.10 | async-start | bytes 2129920 | tf_op jit(solution)/shard_map/all_to_all | solution.py:691
  377.3 3.0 collective-permute-start.6
  (22 other events, 68.1 us)
Sparse Core Ops, SparseCore 0:
  10.2 48.6 all-gather.4
  60.4 44.6 all-gather.6
  106.7 44.5 all-gather.8
  152.7 44.6 all-gather.10
  199.5 76.0 reduce-scatter.2
  279.2 76.6 reduce-scatter.4
